TPU v7x, 256 devices: a whole 4x4x8 slice. The times are simulated.
256 devices in a mesh: gx: 16 (over z_hi, y), gy: 16 (over x, z_lo, core).
Axes of the slice: x: 4, y: 4, z: 8 (z_hi: 4, z_lo: 2; z = z_hi * 2 + z_lo), core: 2. Of those that a mesh axis runs over, the one named last changes fastest.
Arguments:
- flow_state: float32 [4, 48, 256, 2048], P(None, None, 'gx', 'gy'), may hold values from -4 to 4
- inflow: float32 [4, 48, 2048], P(None, None, 'gx'), may hold values from -4 to 4
- footprint: int32 [100, 3], replicated, may hold values from 0 to 2024, as said below
- block_map: int32 [16], replicated, may hold values from 0 to 15, each once
Outputs:
- new_state: float32 [4, 48, 256, 2048], P(None, None, 'gx', 'gy')
Inputs may be any that keep to these rules, and one draw needn't show every extreme that they name: `footprint`: each disk box lies inside the grid and starts at streamwise cell 1 or later. `block_map`: a permutation of the spanwise blocks.
All inputs are finite; a program needn't handle non-finite values.
Results may differ from a plain program's by a relative error of at most 0.00011.
Values sent between devices are 32-bit elements; how exact they have to be, the bound alone decides.
No kernel may reach another device: no remote copies, remote signals or barrier semaphores. Data moves between devices by JAX's collectives and lax.ppermute only.
A program may use at most 64 MiB of HBM per device.

v0:
```python
import jax
import jax.numpy as jnp
from jax import lax
from jax.experimental import pallas as pl
from jax.experimental.pallas import tpu as pltpu
from jax.sharding import PartitionSpec as P

DISK_X = 2
DISK_Y = 24
DISK_Z = 24
CELLS = float(DISK_X * DISK_Y * DISK_Z)

DT = 0.15
VISC = 0.3
BUOY = 0.3
GAIN = 2.0
BASE = DT * VISC
FAR = -100000
F32 = jnp.float32
UNROLL = 16
CHUNK = 8
GROUP = 4
TILE_COST = 1 << 20
PACK_COST = 1 << 33
STEPS_COST = 1 << 32


def pairs(n, odd):
    if not odd:
        return [(i, i ^ 1) for i in range(n)]
    return [(i, (i + 1) % n if i % 2 else (i - 1) % n) for i in range(n)]


def pairs_inside(nx, ny):
    out = []
    for i in range(nx):
        for j in range(ny):
            if i in (0, nx - 1):
                to = (i, j ^ 1)
            else:
                to = (i + 1 if i % 2 else i - 1, j)
            out.append((i * ny + j, to[0] * ny + to[1]))
    return out


def upwind(vel):
    scaled = DT * vel
    return jnp.maximum(scaled, 0.0) + BASE, BASE - jnp.minimum(scaled, 0.0)


def coefs(u, v, w):
    cw, ce = upwind(u)
    cs, cn = upwind(v)
    cb, ca = upwind(w)
    c0 = 1.0 - ((cw + ce) + (cs + cn) + (cb + ca))
    return c0, cw, ce, cs, cn, cb, ca


def mix(c, f, w, e, s, n, b, a):
    return c[0] * f + c[1] * w + c[2] * e + c[3] * s + c[4] * n + c[5] * b + c[6] * a


def dot_nt(a, m):
    high = a.astype(jnp.bfloat16)
    low = (a - high.astype(F32)).astype(jnp.bfloat16)
    dims = (((1,), (1,)), ((), ()))
    return lax.dot_general(high, m, dims, preferred_element_type=F32) + lax.dot_general(
        low, m, dims, preferred_element_type=F32
    )


def dot_nn(a, m):
    high = a.astype(jnp.bfloat16)
    low = (a - high.astype(F32)).astype(jnp.bfloat16)
    return jnp.dot(high, m, preferred_element_type=F32) + jnp.dot(
        low, m, preferred_element_type=F32
    )


def iota(shape, dim):
    return lax.broadcasted_iota(jnp.int32, shape, dim)


def within(cells, start, extent):
    return ((cells >= start) & (cells < start + extent)).astype(F32)


def span_mask(fp, first, count):
    return within(first + iota((count, 128), 0), fp[1:2], DISK_Y).astype(jnp.bfloat16)


def pack_x_kernel(f_ref, a_ref, b_ref, sems):
    even = lax.axis_index("gx") % 2 == 0
    first_a = jnp.where(even, 14, 0)
    first_b = jnp.where(even, 0, 14)
    copies = []
    for c in range(4):
        for i, (first, ref) in enumerate(((first_a, a_ref), (first_b, b_ref))):
            copies.append(
                pltpu.make_async_copy(
                    f_ref.at[c, :, pl.ds(first, 2), :],
                    ref.at[:, pl.ds(2 * c, 2), :],
                    sems.at[c, i],
                )
            )
    for copy in copies:
        copy.start()
    for copy in copies:
        copy.wait()


def pack_inlet_kernel(map_ref, in_ref, after_ref, msg_ref, code_ref):
    nz = in_ref.shape[1]
    lane = iota((1, 128), 1)
    for c in range(4):
        msg_ref[c, 0:nz, :] = in_ref[c]
        msg_ref[c, nz : nz + 8, :] = jnp.zeros((8, 128), F32)
        for half in range(2):
            packed = jnp.zeros((1, 128), F32)
            for z in range(half * 32, min(nz, half * 32 + 32)):
                at = z - half * 32
                moved = pltpu.roll(in_ref[c, z : z + 1, :], (4 * at + 1) % 128, 1)
                packed = jnp.where(lane // 4 == at, moved, packed)
            msg_ref[c, nz + half : nz + half + 1, :] = packed

    tile_y = lax.axis_index("gy")
    count = lax.axis_size("gy")
    place = tile_y % GROUP
    level = iota((nz + 8, 128), 0)
    first = iota((nz + 8, 128), 1) % 4 == 0
    for k in range(GROUP):
        column = tile_y // GROUP * GROUP + (place ^ k)
        own = map_ref[column]
        left = map_ref[(column + count - 1) % count]
        right = map_ref[(column + 1) % count]
        source = jnp.where(level < nz, own, jnp.where(first, left, right))
        source = jnp.where(source == 3, 6, jnp.where(source == 6, 3, source))
        code = source // GROUP
        code = code + jnp.where(source % GROUP == place, 8, 0)
        code_ref[k] = code + jnp.where(source % GROUP // 2 == place // 2, 16, 0)


def pack_y_kernel(f_ref, after_ref, p_ref):
    nz = f_ref.shape[1]
    lane = iota((16, 128), 1)
    p_ref[...] = jnp.zeros_like(p_ref)
    for half in range(2):
        lo, hi = half * 32, min(nz, half * 32 + 32)

        def one(z, packed):
            here = lane // 4 == z - lo
            shift = (2 + 4 * (z - lo)) % 128
            return tuple(
                jnp.where(here, pltpu.roll(f_ref[i, z], shift, 1), packed[i]) for i in range(4)
            )

        zero = jnp.zeros((16, 128), F32)
        packed = lax.fori_loop(lo, hi, one, (zero,) * 4, unroll=UNROLL)
        for i in range(4):
            p_ref[half, i, 0:16, :] = packed[i]


def base_kernel(f_ref, fp_ref, base_ref, disks_ref, sums_ref, rows_ref):
    nz = f_ref.shape[1]
    first_x = lax.axis_index("gx") * 16
    first_y = lax.axis_index("gy") * 128
    fp = fp_ref[...]
    lane = iota((16, 128), 1)
    sub = iota((16, 128), 0)
    mask_x = within(first_x + sub, fp[0:1], DISK_X)

    def one(z, carry):
        below = jnp.maximum(z - 1, 0)
        above = jnp.minimum(z + 1, nz - 1)
        cur = [f_ref[c, z] for c in range(4)]
        c = coefs(cur[0], cur[1], cur[2])
        cw = jnp.where(sub == 0, 0.0, c[1])
        ce = jnp.where(sub == 15, 0.0, c[2])
        cs = jnp.where(lane == 0, 0.0, c[3])
        cn = jnp.where(lane == 127, 0.0, c[4])
        c = (c[0], cw, ce, cs, cn, c[5], c[6])
        for i in range(4):
            f = cur[i]
            new = mix(
                c,
                f,
                pltpu.roll(f, 1, 0),
                pltpu.roll(f, 15, 0),
                pltpu.roll(f, 1, 1),
                pltpu.roll(f, 127, 1),
                f_ref[i, below],
                f_ref[i, above],
            )
            if i == 2:
                new = new + (DT * BUOY) * cur[3]
            base_ref[i, z] = new
        disks_ref[z] = (mask_x * within(z, fp[2:3], DISK_Z)).astype(jnp.bfloat16)
        return carry

    lax.fori_loop(0, nz, one, 0, unroll=UNROLL)
    span = span_mask(fp, first_y, 128)
    rows_ref[0] = dot_nn(f_ref[0].reshape(nz * 16, 128), span).reshape(nz, 16, 128)
    rows_ref[1] = dot_nn(base_ref[0].reshape(nz * 16, 128), span).reshape(nz, 16, 128)

    def add(z, acc):
        mask = within(z, fp[2:3], DISK_Z)
        return acc[0] + rows_ref[0, z] * mask, acc[1] + rows_ref[1, z] * mask

    zero = jnp.zeros((16, 128), F32)
    acc = lax.fori_loop(0, nz, add, (zero, zero), unroll=UNROLL)
    sums_ref[0:1, :] = jnp.sum(acc[0] * mask_x, axis=0, keepdims=True)
    sums_ref[1:2, :] = jnp.sum(acc[1] * mask_x, axis=0, keepdims=True)
    sums_ref[2:8, :] = jnp.zeros((6, 128), F32)


def rim_kernel(
    sa_ref,
    sb_ref,
    ra_ref,
    rb_ref,
    fp_ref,
    sums_ref,
    p_in,
    p_ref,
    cur_ref,
    west_ref,
    east_ref,
    hl_ref,
    hh_ref,
    rows_ref,
):
    nz = hl_ref.shape[0]
    tile_x = lax.axis_index("gx")
    last_x = lax.axis_size("gx") - 1
    even = tile_x % 2 == 0
    first_x = tile_x * 16
    first_y = lax.axis_index("gy") * 128
    fp = fp_ref[...]
    lane = iota((8, 128), 1)
    sub = iota((8, 128), 0)

    @pl.when(even)
    def _():
        hl_ref[...] = rb_ref[...]
        hh_ref[...] = ra_ref[...]

    @pl.when(jnp.logical_not(even))
    def _():
        hl_ref[...] = ra_ref[...]
        hh_ref[...] = rb_ref[...]

    @pl.when(tile_x == 0)
    def _():
        hl_ref[...] = jnp.zeros_like(hl_ref)

    @pl.when(tile_x == last_x)
    def _():
        for z in range(nz):
            hh_ref[z] = pltpu.roll(sb_ref[z], 7, 0)

    def row(x, i):
        return x[i : i + 1]

    for half in range(2):
        lo, hi = half * 32, min(nz, half * 32 + 32)

        def one(z, packed):
            below = jnp.maximum(z - 1, 0)
            above = jnp.minimum(z + 1, nz - 1)
            own_a, own_b = sa_ref[z], sb_ref[z]
            own_low = jnp.where(even, own_b, own_a)
            own_high = jnp.where(even, own_a, own_b)
            low, high = hl_ref[z], hh_ref[z]
            u_low = jnp.where(sub == 0, row(low, 1), row(high, 0))
            v_low = jnp.where(sub == 0, row(low, 3), row(high, 2))
            w_low = jnp.where(sub == 0, row(low, 5), row(high, 4))
            west = jnp.where(sub == 0, row(low, 0), row(own_high, 1))
            east = jnp.where(sub == 0, row(own_low, 0), row(high, 1))
            down = jnp.where(sub == 0, row(hl_ref[below], 1), row(hh_ref[below], 0))
            up = jnp.where(sub == 0, row(hl_ref[above], 1), row(hh_ref[above], 0))
            south = jnp.where(lane == 0, 0.0, pltpu.roll(u_low, 1, 1))
            north = jnp.where(lane == 127, 0.0, pltpu.roll(u_low, 127, 1))
            ring = mix(coefs(u_low, v_low, w_low), u_low, west, east, south, north, down, up)
            into_low = upwind(row(own_low, 0))[0] * row(low, 1)
            into_high = upwind(row(own_high, 1))[1] * row(high, 0)
            both = jnp.where(sub == 2, into_low, jnp.where(sub == 3, into_high, ring))
            both = jnp.where(sub == 4, row(low, 0), both)
            both = jnp.where(sub == 5, row(low, 1), both)
            both = jnp.where(sub == 6, row(high, 0), both)
            both = jnp.where(sub == 7, row(high, 1), both)
            rows_ref[z] = both
            odd = sub % 2 == 1
            cur_ref[z] = jnp.where(odd, low, high)
            west_ref[z] = jnp.where(odd, pltpu.roll(low, 1, 0), pltpu.roll(own_high, 7, 0))
            east_ref[z] = jnp.where(odd, pltpu.roll(own_low, 1, 0), pltpu.roll(high, 7, 0))
            here = lane // 4 == z - lo
            shift = (2 + 4 * (z - lo)) % 128
            return (
                jnp.where(here, pltpu.roll(low, shift, 1), packed[0]),
                jnp.where(here, pltpu.roll(high, shift, 1), packed[1]),
            )

        zero = jnp.zeros((8, 128), F32)
        packed = lax.fori_loop(lo, hi, one, (zero, zero), unroll=UNROLL)
        for c in range(4):
            p_ref[half, c, 0:16, :] = p_in[half, c, 0:16, :]
            p_ref[half, c, 16:17, :] = row(packed[0], 2 * c + 1)
            p_ref[half, c, 17:18, :] = row(packed[1], 2 * c)
            p_ref[half, c, 18:24, :] = jnp.zeros((6, 128), F32)

    span = span_mask(fp, first_y, 128)
    rows_ref[...] = dot_nn(rows_ref[...].reshape(nz * 8, 128), span).reshape(nz, 8, 128)

    def add(z, acc):
        return acc + rows_ref[z] * within(z, fp[2:3], DISK_Z)

    acc = lax.fori_loop(0, nz, add, jnp.zeros((8, 128), F32), unroll=UNROLL)
    column = jnp.where(sub == 0, -1, 16)
    column = jnp.where(sub == 2, 0, jnp.where(sub == 3, 15, column))
    column = jnp.where(sub >= 4, jnp.where(sub < 6, sub - 6, sub + 10), column)
    acc = acc * within(first_x + column, fp[0:1], DISK_X)
    p_ref[0, 0, 18:19, :] = sums_ref[0:1, :] + jnp.sum(acc[4:8], axis=0, keepdims=True)
    p_ref[1, 0, 18:19, :] = sums_ref[1:2, :] + jnp.sum(acc[0:4], axis=0, keepdims=True)


def steps_kernel(
    f_ref,
    base_ref,
    disks_ref,
    cur_ref,
    west_ref,
    east_ref,
    p_ref,
    pa_ref,
    pb_ref,
    fp_ref,
    lap_ref,
    out_ref,
    first_ref,
    first_corner_ref,
    last_ref,
    mid_ref,
    new_ref,
    force_ref,
    rim_force_ref,
    ring_ref,
    edge_ref,
    corner_ref,
    sems,
):
    nz = f_ref.shape[1]
    tile_x = lax.axis_index("gx")
    tile_y = lax.axis_index("gy")
    last_x = lax.axis_size("gx") - 1
    all_y = lax.axis_size("gy") * 128
    even_y = tile_y % 2 == 0
    first_x = tile_x * 16
    first_y = tile_y * 128
    fp = fp_ref[...]
    fx, fy, fz = fp[0:1], fp[1:2], fp[2:3]
    lane = iota((16, 128), 1)
    sub = iota((16, 128), 0)

    def pick(half, c):
        a, b = pa_ref[half, c], pb_ref[half, c]
        return jnp.where(even_y, b, a), jnp.where(even_y, a, b)

    k24 = iota((24, 128), 1) % 4
    left_cols, right_cols = [], []
    for c in range(4):
        lefts, rights = [], []
        for half in range(2):
            left, right = pick(half, c)
            own = p_ref[half, c]
            lefts.append(jnp.where(k24 < 2, left, own))
            rights.append(jnp.where(k24 < 2, own, right))
            edge = jnp.where(k24 == 1, left, pltpu.roll(right, 126, 1))
            edge_ref[0, half, c] = edge[0:16]
            corner_ref[half, 2 * c + 1 : 2 * c + 2, :] = edge[16:17]
            corner_ref[half, 2 * c : 2 * c + 1, :] = edge[17:18]
        left_cols.append(jnp.concatenate(lefts, axis=1))
        right_cols.append(jnp.concatenate(rights, axis=1))
    def total(half):
        left, right = pick(half, 0)
        return p_ref[half, 0, 18:19, :] + left[18:19] + right[18:19]

    def thrust_of(sums):
        speed = sums * (1.0 / CELLS)
        return -GAIN * DT * speed * jnp.abs(speed)

    thrust1 = thrust_of(total(0))
    at = iota((256, 128), 0)
    level = at // 4
    k_at = at % 4
    mask_level = within(level, fz, DISK_Z) * (level < nz).astype(F32)
    y_left = jnp.where(k_at == 1, jnp.where(first_y == 0, all_y - 1, first_y - 1), first_y)
    y_right = jnp.where(
        k_at == 1, first_y + 127, jnp.where(first_y + 128 == all_y, 0, first_y + 128)
    )
    middle = ((k_at == 1) | (k_at == 2)).astype(F32)
    mask_left = mask_level * within(y_left, fy, DISK_Y) * middle
    mask_right = mask_level * within(y_right, fy, DISK_Y) * middle
    k256 = iota((24, 256), 1) % 4

    def facing(cols, mask):
        u, v = cols[0], cols[1]
        cs, cn = upwind(v)
        term = jnp.where(k256 == 1, cn * pltpu.roll(u, 255, 1), cs * pltpu.roll(u, 1, 1))
        term = jnp.concatenate([term, jnp.zeros((8, 256), F32)], axis=0)
        return dot_nn(term, mask.astype(jnp.bfloat16))

    faces = facing(left_cols, mask_left) + facing(right_cols, mask_right)
    sub32 = iota((32, 128), 0)
    column = jnp.where(sub32 == 16, -1, jnp.where(sub32 == 17, 16, sub32))
    mask_x32 = within(first_x + column, fx, DISK_X) * (sub32 < 18).astype(F32)
    faces = jnp.sum(faces * mask_x32, axis=0, keepdims=True)
    pushed = jnp.dot(
        jnp.broadcast_to(thrust1, (8, 128)),
        lap_ref[...],
        precision=lax.Precision.HIGHEST,
        preferred_element_type=F32,
    )
    thrust2 = thrust_of(total(1) + faces + pushed[0:1])

    span = within(first_y + iota((128, 128), 0), fy, DISK_Y)
    disks = disks_ref[...].reshape(nz * 16, 128)

    def dot_disks(mask, weights):
        high = weights.astype(jnp.bfloat16)
        low = (weights - high.astype(F32)).astype(jnp.bfloat16)
        dims = (((1,), (1,)), ((), ()))
        return lax.dot_general(
            mask, high, dims, preferred_element_type=F32
        ) + lax.dot_general(mask, low, dims, preferred_element_type=F32)

    force_ref[0] = dot_disks(disks, span * thrust1).reshape(nz, 16, 128)
    force_ref[1] = dot_disks(disks, span * thrust2).reshape(nz, 16, 128)
    levels = within(iota((nz, 128), 0), fz, DISK_Z).astype(jnp.bfloat16)
    for side, x in ((0, 16), (1, -1)):
        weights = span * (thrust1 * within(first_x + x, fx, DISK_X))
        rim_force_ref[side] = dot_disks(levels, weights)
    by_x1 = within(first_x + sub, fx, DISK_X) * thrust1
    y_cols = jnp.where(k_at == 1, y_left, y_right)
    mask_cols = mask_level * within(y_cols, fy, DISK_Y) * middle
    force_cols = dot_nt(by_x1, mask_cols.astype(jnp.bfloat16))

    lane256 = iota((16, 256), 1)
    sub256 = iota((16, 256), 0)

    def rim_cols(cols):
        cur = [x[0:16] for x in cols]
        c = coefs(cur[0], cur[1], cur[2])
        new = []
        for i in range(4):
            f = cur[i]
            west = jnp.where(sub256 == 0, cols[i][16:17], pltpu.roll(f, 1, 0))
            east = jnp.where(sub256 == 15, cols[i][17:18], pltpu.roll(f, 15, 0))
            south = pltpu.roll(f, 1, 1)
            north = pltpu.roll(f, 255, 1)
            down = jnp.where(lane256 < 4, f, pltpu.roll(f, 4, 1))
            up = jnp.where(lane256 >= 4 * nz - 4, f, pltpu.roll(f, 252, 1))
            new.append(mix(c, f, west, east, south, north, down, up))
        new[0] = new[0] + force_cols
        new[2] = new[2] + (DT * BUOY) * cur[3]
        return new

    left_new, right_new = rim_cols(left_cols), rim_cols(right_cols)
    for c in range(4):
        edge = jnp.where(lane256 % 4 == 1, left_new[c], pltpu.roll(right_new[c], 254, 1))
        edge_ref[1, 0, c] = edge[:, 0:128]
        edge_ref[1, 1, c] = edge[:, 128:256]

    lane8 = iota((8, 128), 1)
    sub8 = iota((8, 128), 0)
    odd = sub8 % 2 == 1

    def rim_rows(z, carry):
        below = jnp.maximum(z - 1, 0)
        above = jnp.minimum(z + 1, nz - 1)
        half = z // 32
        shift = (255 - 4 * (z - 32 * half)) % 128
        cur = cur_ref[z]
        corner = pltpu.roll(corner_ref[half], shift, 1)
        south = jnp.where(lane8 == 0, corner, pltpu.roll(cur, 1, 1))
        north = jnp.where(lane8 == 127, corner, pltpu.roll(cur, 127, 1))
        vel = [jnp.where(odd, cur[2 * i + 1 : 2 * i + 2], cur[2 * i : 2 * i + 1]) for i in range(4)]
        c = coefs(vel[0], vel[1], vel[2])
        new = mix(c, cur, west_ref[z], east_ref[z], south, north, cur_ref[below], cur_ref[above])
        new = new + jnp.where(sub8 // 2 == 2, (DT * BUOY) * vel[3], 0.0)
        new = new + jnp.where(sub8 == 0, rim_force_ref[0, pl.ds(z, 1), :], 0.0)
        new = new + jnp.where(sub8 == 1, rim_force_ref[1, pl.ds(z, 1), :], 0.0)
        ring_ref[z] = jnp.where(odd & (tile_x == 0), cur, new)
        return carry

    lax.fori_loop(0, nz, rim_rows, 0, unroll=UNROLL)

    def first_step(group, carry):
        for j in range(UNROLL):
            z = group * UNROLL + j
            half = z // 32
            shift = (255 - 4 * (z - 32 * half)) % 128
            near = cur_ref[z]
            cw, ce = upwind(f_ref[0, z])
            cs, cn = upwind(f_ref[1, z])
            along_x = jnp.where(sub == 0, cw, jnp.where(sub == 15, ce, 0.0))
            along_y = jnp.where(lane == 0, cs, jnp.where(lane == 127, cn, 0.0))
            for i in range(4):
                beside = jnp.where(sub < 8, near[2 * i + 1 : 2 * i + 2], near[2 * i : 2 * i + 1])
                edge = pltpu.roll(edge_ref[0, half, i], shift, 1)
                new = base_ref[i, z] + along_x * beside + along_y * edge
                if i == 0:
                    new = new + force_ref[0, z]
                mid_ref[i, z] = new
        return carry

    def level(z):
        below = jnp.maximum(z - 1, 0)
        above = jnp.minimum(z + 1, nz - 1)
        half = z // 32
        shift = (255 - 4 * (z - 32 * half)) % 128
        cur = [mid_ref[c, z] for c in range(4)]
        ring = ring_ref[z]
        c = coefs(cur[0], cur[1], cur[2])
        for i in range(4):
            f = cur[i]
            west = jnp.where(sub == 0, ring[2 * i + 1 : 2 * i + 2], pltpu.roll(f, 1, 0))
            outside = jnp.where(tile_x == last_x, f[15:16], ring[2 * i : 2 * i + 1])
            east = jnp.where(sub == 15, outside, pltpu.roll(f, 15, 0))
            edge = pltpu.roll(edge_ref[1, half, i], shift, 1)
            south = jnp.where(lane == 0, edge, pltpu.roll(f, 1, 1))
            north = jnp.where(lane == 127, edge, pltpu.roll(f, 127, 1))
            new = mix(c, f, west, east, south, north, mid_ref[i, below], mid_ref[i, above])
            if i == 0:
                new = new + force_ref[1, z]
            if i == 2:
                new = new + (DT * BUOY) * cur[3]
            new_ref[i, z] = new

    def send(chunk):
        part = pl.ds(chunk * CHUNK, CHUNK)
        return pltpu.make_async_copy(new_ref.at[:, part], out_ref.at[:, part], sems.at[chunk])

    def second_step(group, carry):
        for i in range(UNROLL):
            z = group * UNROLL + i
            level(z)
            if i % CHUNK == CHUNK - 1:
                send(group * (UNROLL // CHUNK) + i // CHUNK).start()
        return carry

    lax.fori_loop(0, nz // UNROLL, first_step, 0)
    lax.fori_loop(0, nz // UNROLL, second_step, 0)

    @pl.when(tile_x == 0)
    def _():
        for c in range(4):
            first_ref[:, 2 * c : 2 * c + 2, :] = mid_ref[c, :, 0:2, :]
            last_ref[:, 2 * c : 2 * c + 2, :] = new_ref[c, :, 0:2, :]
            for half in range(2):
                first_corner_ref[half, 2 * c : 2 * c + 1, :] = edge_ref[1, half, c, 0:1, :]
                first_corner_ref[half, 2 * c + 1 : 2 * c + 2, :] = edge_ref[0, half, c, 0:1, :]

    for chunk in range(nz // CHUNK):
        send(chunk).wait()


def fix_kernel(
    out_in, in_ref, sb_ref, first_ref, corner_ref, last_ref, out_ref, inlet, new, wide, done, sems
):
    nz = first_ref.shape[0]
    lane = iota((8, 128), 1)
    sub = iota((8, 128), 0)
    is_even = sub % 2 == 0


    def send(group):
        part = pl.ds(group * UNROLL, UNROLL)
        return [
            pltpu.make_async_copy(
                done.at[part, pl.ds(2 * c, 2), :], out_ref.at[c, part, pl.ds(0, 2), :], sems.at[group, c]
            )
            for c in range(4)
        ]

    @pl.when(lax.axis_index("gx") == 0)
    def _():
        inlet[...] = jnp.zeros_like(inlet)
        for c in range(4):
            for z in range(nz):
                inlet[z, 2 * c : 2 * c + 1, :] = in_ref[c, z : z + 1, :]
        for half in range(2):
            old = corner_ref[half]
            push = upwind(old[1:2])[0]
            for c in range(4):
                msg = in_ref[c, nz + half : nz + half + 1, :]
                side = jnp.where(
                    lane[0:1] % 4 == 1, pltpu.roll(msg, 1, 1), pltpu.roll(msg, 127, 1)
                )
                wide[half, 2 * c : 2 * c + 1, :] = old[2 * c : 2 * c + 1] + push * side
                wide[half, 2 * c + 1 : 2 * c + 2, :] = jnp.zeros((1, 128), F32)

        def first(group, carry):
            for i in range(UNROLL):
                z = group * UNROLL + i
                push = upwind(sb_ref[z, 0:1, :])[0]
                new[z] = first_ref[z] + jnp.where(is_even, push * inlet[z], 0.0)
            return carry

        lax.fori_loop(0, nz // UNROLL, first, 0)

        def second(group, carry):
            for i in range(UNROLL):
                z = group * UNROLL + i
                below = jnp.maximum(z - 1, 0)
                above = jnp.minimum(z + 1, nz - 1)
                half = z // 32
                shift = (255 - 4 * (z - 32 * half)) % 128
                cur = new[z]
                east = pltpu.roll(cur, 7, 0)
                corner = pltpu.roll(wide[half], shift, 1)
                south = jnp.where(lane == 0, corner, pltpu.roll(cur, 1, 1))
                north = jnp.where(lane == 127, corner, pltpu.roll(cur, 127, 1))
                c = coefs(cur[0:1], cur[2:3], cur[4:5])
                zero = mix(c, cur, inlet[z], east, south, north, new[below], new[above])
                zero = zero + jnp.where(sub == 4, (DT * BUOY) * cur[6:7], 0.0)
                delta = pltpu.roll(cur - first_ref[z], 1, 0)
                one = last_ref[z] + upwind(cur[1:2])[0] * delta
                done[z] = jnp.where(is_even, zero, one)
            for copy in send(group):
                copy.start()
            return carry

        lax.fori_loop(0, nz // UNROLL, second, 0)
        for group in range(nz // UNROLL):
            for copy in send(group):
                copy.wait()


VMEM = pl.BlockSpec(memory_space=pltpu.VMEM)
ANY = pl.BlockSpec(memory_space=pl.ANY)
SMEM = pl.BlockSpec(memory_space=pltpu.SMEM)
HBM = pl.BlockSpec(memory_space=pltpu.HBM)


def call(kernel, out, scratch=(), aliases=None, ins=None, outs=None, flops=1 << 20):
    specs = {}
    if ins is not None:
        specs["in_specs"] = ins
    if outs is not None:
        specs["out_specs"] = outs
    return pl.pallas_call(
        kernel,
        out_shape=out,
        scratch_shapes=scratch,
        input_output_aliases=aliases or {},
        compiler_params=pltpu.CompilerParams(vmem_limit_bytes=24 << 20),
        cost_estimate=pl.CostEstimate(flops=flops, bytes_accessed=1 << 20, transcendentals=0),
        **specs,
    )


def row_of(place):
    return {3: 6, 6: 3}.get(place, place)


def send_inlet(msg, after, count_x, count_y):
    heard = {}
    for m in (2, 3, 1, 0):
        moves = [
            (row_of(GROUP * m + j % GROUP) * count_y + j, j)
            for j in range(count_y)
            if GROUP * m + j % GROUP
        ]
        if m == 0:
            sent, *_ = lax.optimization_barrier((msg, *after))
        else:
            sent = msg
        heard[m] = lax.ppermute(sent, ("gx", "gy"), moves)
    return [heard[m] for m in range(4)]


def share_inlet(msg, heard, code, count_y):
    heard[0] = jnp.where(lax.axis_index("gy") % GROUP == 0, msg, heard[0])

    def pick(k):
        out = heard[0]
        for m in range(1, len(heard)):
            out = jnp.where(code[k] & 7 == m, heard[m], out)
        return out

    core = lax.ppermute(
        jnp.concatenate([pick(1), pick(3)]), "gy", [(j, j ^ 1) for j in range(count_y)]
    )
    mine = jnp.where(code[0] & 8 != 0, pick(0), core[0:4])
    theirs = jnp.where(code[2] & 8 != 0, pick(2), core[4:8])
    other = lax.ppermute(theirs, "gy", [(j, j ^ 2) for j in range(count_y)])
    return jnp.where(code[0] & 16 != 0, mine, other)


def body(flow_state, inflow, footprint, block_map):
    levels = flow_state.shape[1]
    count_x = lax.axis_size("gx")
    count_y = lax.axis_size("gy")
    turbines = footprint.shape[0]
    shape = lambda *s: jax.ShapeDtypeStruct(s, F32)
    x_pack = shape(levels, 8, 128)
    y_pack = shape(2, 4, 24, 128)

    send_a, send_b = call(
        pack_x_kernel, (x_pack, x_pack), [pltpu.SemaphoreType.DMA((4, 2))], ins=[HBM], outs=[VMEM] * 2
    )(flow_state)
    recv_a = lax.ppermute(send_a, "gx", pairs(count_x, False))
    recv_b = lax.ppermute(send_b, ("gx", "gy"), pairs_inside(count_x, count_y))

    late, _ = lax.optimization_barrier((footprint, send_a))
    fp = jnp.pad(late.T, ((0, 5), (0, 128 - turbines)), constant_values=FAR)
    lap = jnp.ones((128, 128), F32)
    for i, extent in enumerate((DISK_X, DISK_Y, DISK_Z)):
        lap = lap * jnp.maximum(extent - jnp.abs(fp[i][:, None] - fp[i][None, :]), 0).astype(F32)
    live = jnp.arange(128) < turbines
    lap = jnp.where(live[:, None] & live[None, :], lap, 0.0)

    own = call(pack_y_kernel, y_pack, flops=PACK_COST)(flow_state, send_a)
    msg, code = call(
        pack_inlet_kernel,
        (shape(4, levels + 8, 128), jax.ShapeDtypeStruct((GROUP, levels + 8, 128), jnp.int32)),
        ins=[SMEM, VMEM, VMEM],
    )(block_map, inflow, own)
    base, disks, sums = call(
        base_kernel,
        (
            shape(*flow_state.shape),
            jax.ShapeDtypeStruct((levels, 16, 128), jnp.bfloat16),
            shape(8, 128),
        ),
        [pltpu.VMEM((2, levels, 16, 128), F32)],
        flops=TILE_COST,
    )(flow_state, fp)
    heard = send_inlet(msg, (recv_b, sums), count_x, count_y)

    own, near, west, east = call(
        rim_kernel, (y_pack, x_pack, x_pack, x_pack), [pltpu.VMEM((levels, 8, 128), F32)] * 3
    )(send_a, send_b, recv_a, recv_b, fp, sums, own)
    side_a = lax.ppermute(own, "gy", pairs(count_y, False))
    side_b = lax.ppermute(own, "gy", pairs(count_y, True))
    *heard, _ = lax.optimization_barrier((*heard, side_b))
    inlet = share_inlet(msg, list(heard), code, count_y)
    out, first, corner, last = call(
        steps_kernel,
        (shape(*flow_state.shape), x_pack, shape(2, 8, 128), x_pack),
        [
            pltpu.VMEM(flow_state.shape, F32),
            pltpu.VMEM(flow_state.shape, F32),
            pltpu.VMEM((2, levels, 16, 128), F32),
            pltpu.VMEM((2, levels, 128), F32),
            pltpu.VMEM((levels, 8, 128), F32),
            pltpu.VMEM((2, 2, 4, 16, 128), F32),
            pltpu.VMEM((2, 8, 128), F32),
            pltpu.SemaphoreType.DMA((levels // CHUNK,)),
        ],
        outs=[ANY, VMEM, VMEM, VMEM],
        flops=STEPS_COST,
    )(flow_state, base, disks, near, west, east, own, side_a, side_b, fp, lap)
    return call(
        fix_kernel,
        shape(*flow_state.shape),
        [
            pltpu.VMEM((levels, 8, 128), F32),
            pltpu.VMEM((levels, 8, 128), F32),
            pltpu.VMEM((2, 8, 128), F32),
            pltpu.VMEM((levels, 8, 128), F32),
            pltpu.SemaphoreType.DMA((levels // UNROLL, 4)),
        ],
        aliases={0: 0},
        ins=[ANY, VMEM, VMEM, VMEM, VMEM, VMEM],
        outs=ANY,
    )(out, inlet, send_b, first, corner, last)


def solution(mesh):
    placed = (P(None, None, "gx", "gy"), P(None, None, "gx"), P(), P())
    return jax.shard_map(
        body, mesh=mesh, in_specs=placed, out_specs=P(None, None, "gx", "gy"), check_vma=False
    )
```

profile of v0, /device:TPU:1, one launch (start us, length us, event | category | flops | bytes accessed | tf_op | source)
XLA Modules:
  0.0 35.2 jit_solution(5932509521706287604)
XLA Ops:
  0.0 0.0 copy-start
  0.0 1.4 %copy-done = f32[4,48,16,128]{3,2,1,0:T(8,128)S(1)} copy-done((f32[4,48,16,128]{3,2,1,0:T(8,128)S(1)}, f32[4,48,16,128]{3,2,1,0:T(8,128)}, u32[]{:S(2)}) %copy-start) | copy-done | bytes 1572888
  1.4 0.2 shard_map.46
  1.6 2.2 %collective-permute-start = (f32[48,8,128]{2,1,0:T(8,128)S(1)}, f32[48,8,128]{2,1,0:T(8,128)S(1)}, u32[]{:S(2)}, u32[]{:S(2)}) collective-permute-start(f32[48,8,128]{2,1,0:T(8,128)S(1)} %get-tuple-element.26.after_ref.sa_ref), channel_id=1, source_target_pairs={{0,16},{16,0},{32,48},{48,32},{64,80},{80,64},{96,112},{112,96},{1... | collective-permute-start | bytes 589832 | tf_op jit(solution)/shard_map/ppermute | solution.py:712
  3.9 0.0 copy-start.2
  3.9 0.0 copy-start.3
  3.9 0.0 copy-start.6
  3.9 0.0 copy-start.1
  3.9 1.3 %collective-permute-start.1 = (f32[48,8,128]{2,1,0:T(8,128)S(1)}, f32[48,8,128]{2,1,0:T(8,128)S(1)}, u32[]{:S(2)}, u32[]{:S(2)}) collective-permute-start(f32[48,8,128]{2,1,0:T(8,128)S(1)} %get-tuple-element.30.sb_ref), channel_id=1, source_target_pairs={{0,1},{1,0},{2,3},{3,2},{4,5},{5,4},{6,7},{7,6},{8,9},{9,8},{10,11... | collective-permute-start | bytes 589832 | tf_op jit(solution)/shard_map/ppermute | solution.py:713
  5.1 0.6 %shard_map.48.p_in.after_ref = f32[2,4,24,128]{3,2,1,0:T(8,128)S(1)} custom-call(f32[4,48,16,128]{3,2,1,0:T(8,128)S(1)} %copy-done, f32[48,8,128]{2,1,0:T(8,128)S(1)} %get-tuple-element.26.after_ref.sa_ref), custom_call_target="tpu_custom_call" | custom-call | flops 8589934592 | bytes 1048576 | tf_op jit(solution)/shard_map/pallas_call | solution.py:723
  5.7 0.0 copy-done.2
  5.7 0.0 copy-done.3
  5.8 0.8 %shard_map.51 = (f32[4,56,128]{2,1,0:T(8,128)S(1)}, s32[4,56,128]{2,1,0:T(8,128)S(1)}) custom-call(s32[16]{0:T(128)S(1)} %copy-done.3, f32[4,48,128]{2,1,0:T(8,128)S(1)} %copy-done.2, f32[2,4,24,128]{3,2,1,0:T(8,128)S(1)} %shard_map.48.p_in.after_ref), custom_call_target="tpu_custom_call" | custom-call | flops 1048576 | bytes 1048576 | tf_op jit(solution)/shard_map/pallas_call | solution.py:724
  6.6 1.3 %collective-permute-start.5 = (f32[4,56,128]{2,1,0:T(8,128)S(1)}, f32[4,56,128]{2,1,0:T(8,128)S(1)}, u32[]{:S(2)}, u32[]{:S(2)}) collective-permute-start(f32[4,56,128]{2,1,0:T(8,128)S(1)} %get-tuple-element.39), channel_id=1, source_target_pairs={{64,0},{81,1},{50,2},{115,3},{68,4},{85,5},{54,6},{119,7},{72,8},{... | collective-permute-start | bytes 344072 | tf_op jit(solution)/shard_map/ppermute | solution.py:678
  7.9 1.3 %collective-permute-start.6 = (f32[4,56,128]{2,1,0:T(8,128)S(1)}, f32[4,56,128]{2,1,0:T(8,128)S(1)}, u32[]{:S(2)}, u32[]{:S(2)}) collective-permute-start(f32[4,56,128]{2,1,0:T(8,128)S(1)} %get-tuple-element.39), channel_id=1, source_target_pairs={{128,0},{145,1},{162,2},{179,3},{132,4},{149,5},{166,6},{183,7},{1... | collective-permute-start | bytes 344072 | tf_op jit(solution)/shard_map/ppermute | solution.py:678
  9.2 1.3 %collective-permute-start.7 = (f32[4,56,128]{2,1,0:T(8,128)S(1)}, f32[4,56,128]{2,1,0:T(8,128)S(1)}, u32[]{:S(2)}, u32[]{:S(2)}) collective-permute-start(f32[4,56,128]{2,1,0:T(8,128)S(1)} %get-tuple-element.39), channel_id=1, source_target_pairs={{192,0},{209,1},{226,2},{243,3},{196,4},{213,5},{230,6},{247,7},{2... | collective-permute-start | bytes 344072 | tf_op jit(solution)/shard_map/ppermute | solution.py:678
  10.5 0.0 copy-done.6
  10.5 0.0 copy-done.1
  10.5 1.9 %shard_map.47 = (f32[4,48,16,128]{3,2,1,0:T(8,128)S(1)}, bf16[48,16,128]{2,1,0:T(8,128)(2,1)S(1)}, f32[8,128]{1,0:T(8,128)S(1)}) custom-call(f32[4,48,16,128]{3,2,1,0:T(8,128)S(1)} %copy-done.1, s32[8,128]{1,0:T(8,128)S(1)} %pad.4.fp_ref), custom_call_target="tpu_custom_call" | custom-call | flops 1048576 | bytes 1048576 | tf_op jit(solution)/shard_map/pallas_call | solution.py:729
  12.4 0.0 copy-start.4
  12.4 1.1 %copy-done.4 = f32[4,48,16,128]{3,2,1,0:T(8,128)} copy-done((f32[4,48,16,128]{3,2,1,0:T(8,128)}, f32[4,48,16,128]{3,2,1,0:T(8,128)S(1)}, u32[]{:S(2)}) %copy-start.4) | copy-done | bytes 1572888
  13.5 0.0 collective-permute-done.1.rb_ref
  13.5 1.3 %collective-permute-start.4 = (f32[4,56,128]{2,1,0:T(8,128)S(1)}, f32[4,56,128]{2,1,0:T(8,128)S(1)}, u32[]{:S(2)}, u32[]{:S(2)}) collective-permute-start(f32[4,56,128]{2,1,0:T(8,128)S(1)} %get-tuple-element.39), channel_id=1, source_target_pairs={{17,1},{34,2},{99,3},{21,5},{38,6},{103,7},{25,9},{42,10},{107,11}... | collective-permute-start | bytes 344072 | tf_op jit(solution)/shard_map/ppermute | solution.py:678
  14.8 0.1 fusion.1
  14.9 0.0 collective-permute-done.ra_ref
  14.9 0.9 %shard_map.49 = (f32[2,4,24,128]{3,2,1,0:T(8,128)S(1)}, f32[48,8,128]{2,1,0:T(8,128)S(1)}, f32[48,8,128]{2,1,0:T(8,128)S(1)}, f32[48,8,128]{2,1,0:T(8,128)S(1)}) custom-call(f32[48,8,128]{2,1,0:T(8,128)S(1)} %get-tuple-element.26.after_ref.sa_ref, f32[48,8,128]{2,1,0:T(8,128)S(1)} %get-tuple-element.30.sb_ref, ...), custom_call_target="tpu_custom_call" | custom-call | flops 1048576 | bytes 1048576 | tf_op jit(solution)/shard_map/pallas_call | solution.py:741
  15.8 0.0 copy-start.5
  15.9 1.5 %collective-permute-start.3 = (f32[2,4,24,128]{3,2,1,0:T(8,128)S(1)}, f32[2,4,24,128]{3,2,1,0:T(8,128)S(1)}, u32[]{:S(2)}, u32[]{:S(2)}) collective-permute-start(f32[2,4,24,128]{3,2,1,0:T(8,128)S(1)} %get-tuple-element.35.p_ref), channel_id=1, source_target_pairs={{0,15},{1,2},{2,1},{3,4},{4,3},{5,6},{6,5},{7,8},{8,7},{9,10},{10,... | collective-permute-start | bytes 294920 | tf_op jit(solution)/shard_map/ppermute | solution.py:745
  17.4 0.0 collective-permute-done.5
  17.4 1.2 %collective-permute-done.6 = f32[4,56,128]{2,1,0:T(8,128)S(1)} collective-permute-done((f32[4,56,128]{2,1,0:T(8,128)S(1)}, f32[4,56,128]{2,1,0:T(8,128)S(1)}, u32[]{:S(2)}, u32[]{:S(2)}) %collective-permute-start.6) | collective-permute-done | bytes 114720 | tf_op jit(solution)/shard_map/ppermute | solution.py:678
  18.6 0.9 %collective-permute-done.7 = f32[4,56,128]{2,1,0:T(8,128)S(1)} collective-permute-done((f32[4,56,128]{2,1,0:T(8,128)S(1)}, f32[4,56,128]{2,1,0:T(8,128)S(1)}, u32[]{:S(2)}, u32[]{:S(2)}) %collective-permute-start.7) | collective-permute-done | bytes 114720 | tf_op jit(solution)/shard_map/ppermute | solution.py:678
  19.6 1.4 %collective-permute-done.3.pb_ref = f32[2,4,24,128]{3,2,1,0:T(8,128)S(1)} collective-permute-done((f32[2,4,24,128]{3,2,1,0:T(8,128)S(1)}, f32[2,4,24,128]{3,2,1,0:T(8,128)S(1)}, u32[]{:S(2)}, u32[]{:S(2)}) %collective-permute-start.3) | collective-permute-done | bytes 98336 | tf_op jit(solution)/shard_map/ppermute | solution.py:745
  20.9 0.1 collective-permute-done.4
  21.1 2.4 %collective-permute-start.8 = (f32[8,56,128]{2,1,0:T(8,128)S(1)}, f32[8,56,128]{2,1,0:T(8,128)S(1)}, u32[]{:S(2)}, u32[]{:S(2)}) collective-permute-start(f32[8,56,128]{2,1,0:T(8,128)S(1)} %pad_maximum_fusion), channel_id=1, source_target_pairs={{0,1},{1,0},{2,3},{3,2},{4,5},{5,4},{6,7},{7,6},{8,9},{9,8},{10,11... | collective-permute-start | bytes 688136 | tf_op jit(solution)/shard_map/ppermute | solution.py:691
  23.5 0.1 multiply_select_fusion.lap_ref
  23.7 0.1 collective-permute-start.2
  23.8 0.9 %collective-permute-done.8 = f32[8,56,128]{2,1,0:T(8,128)S(1)} collective-permute-done((f32[8,56,128]{2,1,0:T(8,128)S(1)}, f32[8,56,128]{2,1,0:T(8,128)S(1)}, u32[]{:S(2)}, u32[]{:S(2)}) %collective-permute-start.8) | collective-permute-done | bytes 229408 | tf_op jit(solution)/shard_map/ppermute | solution.py:691
  24.7 3.9 %collective-permute-start.9 = (f32[4,56,128]{2,1,0:T(8,128)S(1)}, f32[4,56,128]{2,1,0:T(8,128)S(1)}, u32[]{:S(2)}, u32[]{:S(2)}) collective-permute-start(f32[4,56,128]{2,1,0:T(8,128)S(1)} %slice_select_fusion), channel_id=1, source_target_pairs={{0,2},{1,3},{2,0},{3,1},{4,6},{5,7},{6,4},{7,5},{8,10},{9,11},{10,... | collective-permute-start | bytes 344072 | tf_op jit(solution)/shard_map/ppermute | solution.py:696
  28.6 0.0 collective-permute-done.2.pa_ref
  28.6 0.0 copy-done.5
  28.6 4.9 %shard_map.50 = (f32[4,48,16,128]{3,2,1,0:T(8,128)}, f32[48,8,128]{2,1,0:T(8,128)S(1)}, f32[2,8,128]{2,1,0:T(8,128)S(1)}, f32[48,8,128]{2,1,0:T(8,128)S(1)}) custom-call(f32[4,48,16,128]{3,2,1,0:T(8,128)S(1)} %copy-done.1, f32[4,48,16,128]{3,2,1,0:T(8,128)S(1)} %copy-done.5, bf16[48,16,128]{2,1,0:T(8,128)(2,1)S(1)} %get-tuple-element.29.disks_ref, ...), custom_call_target="tpu_custom_call" | custom-call | flops 4294967296 | bytes 1048576 | tf_op jit(solution)/shard_map/pallas_call | solution.py:748
  33.5 0.0 collective-permute-done.9
  33.5 1.6 %shard_map.52 = f32[4,48,16,128]{3,2,1,0:T(8,128)} custom-call(f32[4,48,16,128]{3,2,1,0:T(8,128)} %get-tuple-element.36.out_in, f32[4,56,128]{2,1,0:T(8,128)S(1)} %fusion.in_ref, f32[48,8,128]{2,1,0:T(8,128)S(1)} %get-tuple-element.30.sb_ref, f32[48,8,128]{2,1,0:T(8,128)S(1)} %get-tuple-element.44.first_ref, ...), custom_call_target="tpu_custom_call", output_to_operand_aliasing={{}: (0, {})} | custom-call | flops 1048576 | bytes 1048576 | tf_op jit(solution)/shard_map/pallas_call | solution.py:764
  (8 shorter events, 0.2 us)
Async XLA Ops:
  0.0 1.4 %copy-start = (f32[4,48,16,128]{3,2,1,0:T(8,128)S(1)}, f32[4,48,16,128]{3,2,1,0:T(8,128)}, u32[]{:S(2)}) copy-start(f32[4,48,16,128]{3,2,1,0:T(8,128)} %f_ref.7) | copy-start | bytes 4718596
  1.6 13.3 %collective-permute-start = (f32[48,8,128]{2,1,0:T(8,128)S(1)}, f32[48,8,128]{2,1,0:T(8,128)S(1)}, u32[]{:S(2)}, u32[]{:S(2)}) collective-permute-start(f32[48,8,128]{2,1,0:T(8,128)S(1)} %get-tuple-element.26.after_ref.sa_ref), channel_id=1, source_target_pairs={{0,16},{16,0},{32,48},{48,32},{64,80},{80,64},{96,112},{112,96},{1... | collective-permute-start | bytes 589832 | tf_op jit(solution)/shard_map/ppermute | solution.py:712
  3.9 1.9 %copy-start.2 = (f32[4,48,128]{2,1,0:T(8,128)S(1)}, f32[4,48,128]{2,1,0:T(8,128)}, u32[]{:S(2)}) copy-start(f32[4,48,128]{2,1,0:T(8,128)} %in_ref.1) | copy-start | bytes 294916
  3.9 1.9 %copy-start.3 = (s32[16]{0:T(128)S(1)}, s32[16]{0:T(128)}, u32[]{:S(2)}) copy-start(s32[16]{0:T(128)} %map_ref.1) | copy-start | bytes 196
  3.9 6.6 %copy-start.6 = (s32[100,3]{0,1:T(4,128)S(1)}, s32[100,3]{0,1:T(4,128)}, u32[]{:S(2)}) copy-start(s32[100,3]{0,1:T(4,128)} %param.6) | copy-start | bytes 3604
  3.9 6.6 %copy-start.1 = (f32[4,48,16,128]{3,2,1,0:T(8,128)S(1)}, f32[4,48,16,128]{3,2,1,0:T(8,128)}, u32[]{:S(2)}) copy-start(f32[4,48,16,128]{3,2,1,0:T(8,128)} %f_ref.7) | copy-start | bytes 4718596
  3.9 9.7 %collective-permute-start.1 = (f32[48,8,128]{2,1,0:T(8,128)S(1)}, f32[48,8,128]{2,1,0:T(8,128)S(1)}, u32[]{:S(2)}, u32[]{:S(2)}) collective-permute-start(f32[48,8,128]{2,1,0:T(8,128)S(1)} %get-tuple-element.30.sb_ref), channel_id=1, source_target_pairs={{0,1},{1,0},{2,3},{3,2},{4,5},{5,4},{6,7},{7,6},{8,9},{9,8},{10,11... | collective-permute-start | bytes 589832 | tf_op jit(solution)/shard_map/ppermute | solution.py:713
  6.6 10.8 %collective-permute-start.5 = (f32[4,56,128]{2,1,0:T(8,128)S(1)}, f32[4,56,128]{2,1,0:T(8,128)S(1)}, u32[]{:S(2)}, u32[]{:S(2)}) collective-permute-start(f32[4,56,128]{2,1,0:T(8,128)S(1)} %get-tuple-element.39), channel_id=1, source_target_pairs={{64,0},{81,1},{50,2},{115,3},{68,4},{85,5},{54,6},{119,7},{72,8},{... | collective-permute-start | bytes 344072 | tf_op jit(solution)/shard_map/ppermute | solution.py:678
  7.9 10.8 %collective-permute-start.6 = (f32[4,56,128]{2,1,0:T(8,128)S(1)}, f32[4,56,128]{2,1,0:T(8,128)S(1)}, u32[]{:S(2)}, u32[]{:S(2)}) collective-permute-start(f32[4,56,128]{2,1,0:T(8,128)S(1)} %get-tuple-element.39), channel_id=1, source_target_pairs={{128,0},{145,1},{162,2},{179,3},{132,4},{149,5},{166,6},{183,7},{1... | collective-permute-start | bytes 344072 | tf_op jit(solution)/shard_map/ppermute | solution.py:678
  9.2 10.4 %collective-permute-start.7 = (f32[4,56,128]{2,1,0:T(8,128)S(1)}, f32[4,56,128]{2,1,0:T(8,128)S(1)}, u32[]{:S(2)}, u32[]{:S(2)}) collective-permute-start(f32[4,56,128]{2,1,0:T(8,128)S(1)} %get-tuple-element.39), channel_id=1, source_target_pairs={{192,0},{209,1},{226,2},{243,3},{196,4},{213,5},{230,6},{247,7},{2... | collective-permute-start | bytes 344072 | tf_op jit(solution)/shard_map/ppermute | solution.py:678
  12.4 1.1 %copy-start.4 = (f32[4,48,16,128]{3,2,1,0:T(8,128)}, f32[4,48,16,128]{3,2,1,0:T(8,128)S(1)}, u32[]{:S(2)}) copy-start(f32[4,48,16,128]{3,2,1,0:T(8,128)S(1)} %get-tuple-element.28.base_ref) | copy-start | bytes 4718596
  13.5 7.5 %collective-permute-start.4 = (f32[4,56,128]{2,1,0:T(8,128)S(1)}, f32[4,56,128]{2,1,0:T(8,128)S(1)}, u32[]{:S(2)}, u32[]{:S(2)}) collective-permute-start(f32[4,56,128]{2,1,0:T(8,128)S(1)} %get-tuple-element.39), channel_id=1, source_target_pairs={{17,1},{34,2},{99,3},{21,5},{38,6},{103,7},{25,9},{42,10},{107,11}... | collective-permute-start | bytes 344072 | tf_op jit(solution)/shard_map/ppermute | solution.py:678
  15.8 12.8 %copy-start.5 = (f32[4,48,16,128]{3,2,1,0:T(8,128)S(1)}, f32[4,48,16,128]{3,2,1,0:T(8,128)}, u32[]{:S(2)}) copy-start(f32[4,48,16,128]{3,2,1,0:T(8,128)} %copy-done.4) | copy-start | bytes 4718596
  15.9 5.1 %collective-permute-start.3 = (f32[2,4,24,128]{3,2,1,0:T(8,128)S(1)}, f32[2,4,24,128]{3,2,1,0:T(8,128)S(1)}, u32[]{:S(2)}, u32[]{:S(2)}) collective-permute-start(f32[2,4,24,128]{3,2,1,0:T(8,128)S(1)} %get-tuple-element.35.p_ref), channel_id=1, source_target_pairs={{0,15},{1,2},{2,1},{3,4},{4,3},{5,6},{6,5},{7,8},{8,7},{9,10},{10,... | collective-permute-start | bytes 294920 | tf_op jit(solution)/shard_map/ppermute | solution.py:745
  21.1 3.6 %collective-permute-start.8 = (f32[8,56,128]{2,1,0:T(8,128)S(1)}, f32[8,56,128]{2,1,0:T(8,128)S(1)}, u32[]{:S(2)}, u32[]{:S(2)}) collective-permute-start(f32[8,56,128]{2,1,0:T(8,128)S(1)} %pad_maximum_fusion), channel_id=1, source_target_pairs={{0,1},{1,0},{2,3},{3,2},{4,5},{5,4},{6,7},{7,6},{8,9},{9,8},{10,11... | collective-permute-start | bytes 688136 | tf_op jit(solution)/shard_map/ppermute | solution.py:691
  23.7 4.9 %collective-permute-start.2 = (f32[2,4,24,128]{3,2,1,0:T(8,128)S(1)}, f32[2,4,24,128]{3,2,1,0:T(8,128)S(1)}, u32[]{:S(2)}, u32[]{:S(2)}) collective-permute-start(f32[2,4,24,128]{3,2,1,0:T(8,128)S(1)} %get-tuple-element.35.p_ref), channel_id=1, source_target_pairs={{0,1},{1,0},{2,3},{3,2},{4,5},{5,4},{6,7},{7,6},{8,9},{9,8},{10,11... | collective-permute-start | bytes 294920 | tf_op jit(solution)/shard_map/ppermute | solution.py:744
  24.7 8.8 %collective-permute-start.9 = (f32[4,56,128]{2,1,0:T(8,128)S(1)}, f32[4,56,128]{2,1,0:T(8,128)S(1)}, u32[]{:S(2)}, u32[]{:S(2)}) collective-permute-start(f32[4,56,128]{2,1,0:T(8,128)S(1)} %slice_select_fusion), channel_id=1, source_target_pairs={{0,2},{1,3},{2,0},{3,1},{4,6},{5,7},{6,4},{7,5},{8,10},{9,11},{10,... | collective-permute-start | bytes 344072 | tf_op jit(solution)/shard_map/ppermute | solution.py:696
where the time goes:
time: 35.4 us; the launch traced here: 35.2 us
  starting transfers between devices  16.6 us (47%)
  Pallas kernels  10.9 us (31%)
  waiting for transfers between devices  4.45 us (13%)
  local copies, waits for them, and re-layouts  2.58 us (7%)
  other arithmetic  0.37 us (1%)
    ppermute x4, starting transfers between devices, send_inlet(): heard[m] = lax.ppermute(sent, ('gx', 'gy'), moves)  5.16 us
    pallas_call x1, Pallas kernels, body(): call(steps_kernel, (shape(*flow_state.shape), x_pack, shape(2, 8, 128), x...  4.86 us
    ppermute x1, starting transfers between devices, share_inlet(): other = lax.ppermute(theirs, 'gy', [(j, j ^ 2) for j in range(count_y)])  3.92 us
    unnamed x14, local copies, waits for them, and re-layouts  2.57 us
    ppermute x1, starting transfers between devices, share_inlet(): lax.ppermute(jnp.concatenate([pick(1), pick(3)]), 'gy', [(j, j ^ 1) for j...  2.44 us
    ppermute x4, waiting for transfers between devices, send_inlet(): heard[m] = lax.ppermute(sent, ('gx', 'gy'), moves)  2.23 us
    ppermute x1, starting transfers between devices, body(): recv_a = lax.ppermute(send_a, 'gx', pairs(count_x, False))  2.21 us
    pallas_call x1, Pallas kernels, body(): call(base_kernel, (shape(*flow_state.shape), jax.ShapeDtypeStruct((levels...  1.87 us
  transfers between devices with their start and end apart: 10, of which 5 were waited for; matrix products, arithmetic and copies ran while one was open for 1% of the time, Pallas kernels for 26%

commit v1 on v0

--- a/solution.py
+++ b/solution.py
@@ -18,6 +18,8 @@
 FAR = -100000
 F32 = jnp.float32
 UNROLL = 16
+WIDE = 24
+TRADES = ((2, 5), (3, 13))
 CHUNK = 8
 GROUP = 4
 TILE_COST = 1 << 20
@@ -134,7 +136,10 @@
         left = map_ref[(column + count - 1) % count]
         right = map_ref[(column + 1) % count]
         source = jnp.where(level < nz, own, jnp.where(first, left, right))
-        source = jnp.where(source == 3, 6, jnp.where(source == 6, 3, source))
+        moved = source
+        for one, two in TRADES:
+            moved = jnp.where(source == one, two, jnp.where(source == two, one, moved))
+        source = moved
         code = source // GROUP
         code = code + jnp.where(source % GROUP == place, 8, 0)
         code_ref[k] = code + jnp.where(source % GROUP // 2 == place // 2, 16, 0)
@@ -197,7 +202,7 @@
         disks_ref[z] = (mask_x * within(z, fp[2:3], DISK_Z)).astype(jnp.bfloat16)
         return carry
 
-    lax.fori_loop(0, nz, one, 0, unroll=UNROLL)
+    lax.fori_loop(0, nz, one, 0, unroll=WIDE)
     span = span_mask(fp, first_y, 128)
     rows_ref[0] = dot_nn(f_ref[0].reshape(nz * 16, 128), span).reshape(nz, 16, 128)
     rows_ref[1] = dot_nn(base_ref[0].reshape(nz * 16, 128), span).reshape(nz, 16, 128)
@@ -207,7 +212,7 @@
         return acc[0] + rows_ref[0, z] * mask, acc[1] + rows_ref[1, z] * mask
 
     zero = jnp.zeros((16, 128), F32)
-    acc = lax.fori_loop(0, nz, add, (zero, zero), unroll=UNROLL)
+    acc = lax.fori_loop(0, nz, add, (zero, zero), unroll=WIDE)
     sums_ref[0:1, :] = jnp.sum(acc[0] * mask_x, axis=0, keepdims=True)
     sums_ref[1:2, :] = jnp.sum(acc[1] * mask_x, axis=0, keepdims=True)
     sums_ref[2:8, :] = jnp.zeros((6, 128), F32)
@@ -314,7 +319,7 @@
     def add(z, acc):
         return acc + rows_ref[z] * within(z, fp[2:3], DISK_Z)
 
-    acc = lax.fori_loop(0, nz, add, jnp.zeros((8, 128), F32), unroll=UNROLL)
+    acc = lax.fori_loop(0, nz, add, jnp.zeros((8, 128), F32), unroll=WIDE)
     column = jnp.where(sub == 0, -1, 16)
     column = jnp.where(sub == 2, 0, jnp.where(sub == 3, 15, column))
     column = jnp.where(sub >= 4, jnp.where(sub < 6, sub - 6, sub + 10), column)
@@ -492,11 +497,11 @@
         ring_ref[z] = jnp.where(odd & (tile_x == 0), cur, new)
         return carry
 
-    lax.fori_loop(0, nz, rim_rows, 0, unroll=UNROLL)
+    lax.fori_loop(0, nz, rim_rows, 0, unroll=WIDE)
 
     def first_step(group, carry):
-        for j in range(UNROLL):
-            z = group * UNROLL + j
+        for j in range(WIDE):
+            z = group * WIDE + j
             half = z // 32
             shift = (255 - 4 * (z - 32 * half)) % 128
             near = cur_ref[z]
@@ -541,15 +546,15 @@
         return pltpu.make_async_copy(new_ref.at[:, part], out_ref.at[:, part], sems.at[chunk])
 
     def second_step(group, carry):
-        for i in range(UNROLL):
-            z = group * UNROLL + i
+        for i in range(WIDE):
+            z = group * WIDE + i
             level(z)
             if i % CHUNK == CHUNK - 1:
-                send(group * (UNROLL // CHUNK) + i // CHUNK).start()
+                send(group * (WIDE // CHUNK) + i // CHUNK).start()
         return carry
 
-    lax.fori_loop(0, nz // UNROLL, first_step, 0)
-    lax.fori_loop(0, nz // UNROLL, second_step, 0)
+    lax.fori_loop(0, nz // WIDE, first_step, 0)
+    lax.fori_loop(0, nz // WIDE, second_step, 0)
 
     @pl.when(tile_x == 0)
     def _():
@@ -574,7 +579,7 @@
 
 
     def send(group):
-        part = pl.ds(group * UNROLL, UNROLL)
+        part = pl.ds(group * WIDE, WIDE)
         return [
             pltpu.make_async_copy(
                 done.at[part, pl.ds(2 * c, 2), :], out_ref.at[c, part, pl.ds(0, 2), :], sems.at[group, c]
@@ -600,17 +605,17 @@
                 wide[half, 2 * c + 1 : 2 * c + 2, :] = jnp.zeros((1, 128), F32)
 
         def first(group, carry):
-            for i in range(UNROLL):
-                z = group * UNROLL + i
+            for i in range(WIDE):
+                z = group * WIDE + i
                 push = upwind(sb_ref[z, 0:1, :])[0]
                 new[z] = first_ref[z] + jnp.where(is_even, push * inlet[z], 0.0)
             return carry
 
-        lax.fori_loop(0, nz // UNROLL, first, 0)
+        lax.fori_loop(0, nz // WIDE, first, 0)
 
         def second(group, carry):
-            for i in range(UNROLL):
-                z = group * UNROLL + i
+            for i in range(WIDE):
+                z = group * WIDE + i
                 below = jnp.maximum(z - 1, 0)
                 above = jnp.minimum(z + 1, nz - 1)
                 half = z // 32
@@ -630,8 +635,8 @@
                 copy.start()
             return carry
 
-        lax.fori_loop(0, nz // UNROLL, second, 0)
-        for group in range(nz // UNROLL):
+        lax.fori_loop(0, nz // WIDE, second, 0)
+        for group in range(nz // WIDE):
             for copy in send(group):
                 copy.wait()
 
@@ -660,7 +665,10 @@
 
 
 def row_of(place):
-    return {3: 6, 6: 3}.get(place, place)
+    for one, two in TRADES:
+        if place in (one, two):
+            return one + two - place
+    return place
 
 
 def send_inlet(msg, after, count_x, count_y):
@@ -769,7 +777,7 @@
             pltpu.VMEM((levels, 8, 128), F32),
             pltpu.VMEM((2, 8, 128), F32),
             pltpu.VMEM((levels, 8, 128), F32),
-            pltpu.SemaphoreType.DMA((levels // UNROLL, 4)),
+            pltpu.SemaphoreType.DMA((levels // WIDE, 4)),
         ],
         aliases={0: 0},
         ins=[ANY, VMEM, VMEM, VMEM, VMEM, VMEM],

time: 35.4 us -> 34 us (0.960)
  the two profiles are of different devices: /device:TPU:1 before, /device:TPU:161 now
where the time goes in v1:
time: 34 us; the launch traced here: 33.8 us
  starting transfers between devices  13.9 us (41%)
  Pallas kernels  9.19 us (27%)
  waiting for transfers between devices  7.46 us (22%)
  local copies, waits for them, and re-layouts  2.58 us (8%)
  other arithmetic  0.37 us (1%)
    pallas_call x1, Pallas kernels, body(): call(steps_kernel, (shape(*flow_state.shape), x_pack, shape(2, 8, 128), x...  4.7 us
    ppermute x1, starting transfers between devices, body(): side_b = lax.ppermute(own, 'gy', pairs(count_y, True))  4.5 us
    ppermute x1, waiting for transfers between devices, body(): recv_b = lax.ppermute(send_b, ('gx', 'gy'), pairs_inside(count_x, count_y))  4.43 us
    ppermute x1, starting transfers between devices, share_inlet(): other = lax.ppermute(theirs, 'gy', [(j, j ^ 2) for j in range(count_y)])  2.76 us
    ppermute x4, starting transfers between devices, send_inlet(): heard[m] = lax.ppermute(sent, ('gx', 'gy'), moves)  2.66 us
    unnamed x14, local copies, waits for them, and re-layouts  2.57 us
    ppermute x1, waiting for transfers between devices, body(): side_b = lax.ppermute(own, 'gy', pairs(count_y, True))  2.27 us
    ppermute x1, starting transfers between devices, body(): recv_b = lax.ppermute(send_b, ('gx', 'gy'), pairs_inside(count_x, count_y))  1.98 us
  transfers between devices with their start and end apart: 10, of which 3 were waited for; matrix products, arithmetic and copies ran while one was open for 1% of the time, Pallas kernels for 26%

profile of v1, /device:TPU:161, one launch (start us, length us, event | category | flops | bytes accessed | tf_op | source)
XLA Modules:
  0.0 33.8 jit_solution(13191471782256247517)
XLA Ops:
  0.0 0.0 copy-start
  0.0 1.4 %copy-done = f32[4,48,16,128]{3,2,1,0:T(8,128)S(1)} copy-done((f32[4,48,16,128]{3,2,1,0:T(8,128)S(1)}, f32[4,48,16,128]{3,2,1,0:T(8,128)}, u32[]{:S(2)}) %copy-start) | copy-done | bytes 1572888
  1.4 0.2 shard_map.46
  1.6 1.4 %collective-permute-start = (f32[48,8,128]{2,1,0:T(8,128)S(1)}, f32[48,8,128]{2,1,0:T(8,128)S(1)}, u32[]{:S(2)}, u32[]{:S(2)}) collective-permute-start(f32[48,8,128]{2,1,0:T(8,128)S(1)} %get-tuple-element.26.after_ref.sa_ref), channel_id=1, source_target_pairs={{0,16},{16,0},{32,48},{48,32},{64,80},{80,64},{96,112},{112,96},{1... | collective-permute-start | bytes 589832 | tf_op jit(solution)/shard_map/ppermute | solution.py:720
  3.0 0.0 copy-start.2
  3.0 0.0 copy-start.3
  3.0 0.0 copy-start.6
  3.0 0.0 copy-start.1
  3.0 2.0 %collective-permute-start.1 = (f32[48,8,128]{2,1,0:T(8,128)S(1)}, f32[48,8,128]{2,1,0:T(8,128)S(1)}, u32[]{:S(2)}, u32[]{:S(2)}) collective-permute-start(f32[48,8,128]{2,1,0:T(8,128)S(1)} %get-tuple-element.30.sb_ref), channel_id=1, source_target_pairs={{0,1},{1,0},{2,3},{3,2},{4,5},{5,4},{6,7},{7,6},{8,9},{9,8},{10,11... | collective-permute-start | bytes 589832 | tf_op jit(solution)/shard_map/ppermute | solution.py:721
  5.0 0.6 %shard_map.48.p_in.after_ref = f32[2,4,24,128]{3,2,1,0:T(8,128)S(1)} custom-call(f32[4,48,16,128]{3,2,1,0:T(8,128)S(1)} %copy-done, f32[48,8,128]{2,1,0:T(8,128)S(1)} %get-tuple-element.26.after_ref.sa_ref), custom_call_target="tpu_custom_call" | custom-call | flops 8589934592 | bytes 1048576 | tf_op jit(solution)/shard_map/pallas_call | solution.py:731
  5.6 0.0 copy-done.2
  5.6 0.0 copy-done.3
  5.7 0.8 %shard_map.51 = (f32[4,56,128]{2,1,0:T(8,128)S(1)}, s32[4,56,128]{2,1,0:T(8,128)S(1)}) custom-call(s32[16]{0:T(128)S(1)} %copy-done.3, f32[4,48,128]{2,1,0:T(8,128)S(1)} %copy-done.2, f32[2,4,24,128]{3,2,1,0:T(8,128)S(1)} %shard_map.48.p_in.after_ref), custom_call_target="tpu_custom_call" | custom-call | flops 1048576 | bytes 1048576 | tf_op jit(solution)/shard_map/pallas_call | solution.py:732
  6.5 0.7 %collective-permute-start.5 = (f32[4,56,128]{2,1,0:T(8,128)S(1)}, f32[4,56,128]{2,1,0:T(8,128)S(1)}, u32[]{:S(2)}, u32[]{:S(2)}) collective-permute-start(f32[4,56,128]{2,1,0:T(8,128)S(1)} %get-tuple-element.39), channel_id=1, source_target_pairs={{64,0},{33,1},{98,2},{115,3},{68,4},{37,5},{102,6},{119,7},{72,8},... | collective-permute-start | bytes 344072 | tf_op jit(solution)/shard_map/ppermute | solution.py:686
  7.1 0.7 %collective-permute-start.6 = (f32[4,56,128]{2,1,0:T(8,128)S(1)}, f32[4,56,128]{2,1,0:T(8,128)S(1)}, u32[]{:S(2)}, u32[]{:S(2)}) collective-permute-start(f32[4,56,128]{2,1,0:T(8,128)S(1)} %get-tuple-element.39), channel_id=1, source_target_pairs={{128,0},{145,1},{162,2},{179,3},{132,4},{149,5},{166,6},{183,7},{1... | collective-permute-start | bytes 344072 | tf_op jit(solution)/shard_map/ppermute | solution.py:686
  7.8 0.7 %collective-permute-start.7 = (f32[4,56,128]{2,1,0:T(8,128)S(1)}, f32[4,56,128]{2,1,0:T(8,128)S(1)}, u32[]{:S(2)}, u32[]{:S(2)}) collective-permute-start(f32[4,56,128]{2,1,0:T(8,128)S(1)} %get-tuple-element.39), channel_id=1, source_target_pairs={{192,0},{49,1},{226,2},{243,3},{196,4},{53,5},{230,6},{247,7},{200... | collective-permute-start | bytes 344072 | tf_op jit(solution)/shard_map/ppermute | solution.py:686
  8.5 0.0 copy-done.6
  8.5 0.0 copy-done.1
  8.5 1.8 %shard_map.47 = (f32[4,48,16,128]{3,2,1,0:T(8,128)S(1)}, bf16[48,16,128]{2,1,0:T(8,128)(2,1)S(1)}, f32[8,128]{1,0:T(8,128)S(1)}) custom-call(f32[4,48,16,128]{3,2,1,0:T(8,128)S(1)} %copy-done.1, s32[8,128]{1,0:T(8,128)S(1)} %pad.4.fp_ref), custom_call_target="tpu_custom_call" | custom-call | flops 1048576 | bytes 1048576 | tf_op jit(solution)/shard_map/pallas_call | solution.py:737
  10.4 0.0 copy-start.4
  10.4 1.1 %copy-done.4 = f32[4,48,16,128]{3,2,1,0:T(8,128)} copy-done((f32[4,48,16,128]{3,2,1,0:T(8,128)}, f32[4,48,16,128]{3,2,1,0:T(8,128)S(1)}, u32[]{:S(2)}) %copy-start.4) | copy-done | bytes 1572888
  11.5 4.4 %collective-permute-done.1.rb_ref = f32[48,8,128]{2,1,0:T(8,128)S(1)} collective-permute-done((f32[48,8,128]{2,1,0:T(8,128)S(1)}, f32[48,8,128]{2,1,0:T(8,128)S(1)}, u32[]{:S(2)}, u32[]{:S(2)}) %collective-permute-start.1) | collective-permute-done | bytes 196640 | tf_op jit(solution)/shard_map/ppermute | solution.py:721
  15.9 0.7 %collective-permute-start.4 = (f32[4,56,128]{2,1,0:T(8,128)S(1)}, f32[4,56,128]{2,1,0:T(8,128)S(1)}, u32[]{:S(2)}, u32[]{:S(2)}) collective-permute-start(f32[4,56,128]{2,1,0:T(8,128)S(1)} %get-tuple-element.39), channel_id=1, source_target_pairs={{17,1},{82,2},{211,3},{21,5},{86,6},{215,7},{25,9},{90,10},{219,11... | collective-permute-start | bytes 344072 | tf_op jit(solution)/shard_map/ppermute | solution.py:686
  16.6 0.1 fusion.1
  16.7 0.0 collective-permute-done.ra_ref
  16.7 0.9 %shard_map.49 = (f32[2,4,24,128]{3,2,1,0:T(8,128)S(1)}, f32[48,8,128]{2,1,0:T(8,128)S(1)}, f32[48,8,128]{2,1,0:T(8,128)S(1)}, f32[48,8,128]{2,1,0:T(8,128)S(1)}) custom-call(f32[48,8,128]{2,1,0:T(8,128)S(1)} %get-tuple-element.26.after_ref.sa_ref, f32[48,8,128]{2,1,0:T(8,128)S(1)} %get-tuple-element.30.sb_ref, ...), custom_call_target="tpu_custom_call" | custom-call | flops 1048576 | bytes 1048576 | tf_op jit(solution)/shard_map/pallas_call | solution.py:749
  17.6 0.0 copy-start.5
  17.6 4.5 %collective-permute-start.3 = (f32[2,4,24,128]{3,2,1,0:T(8,128)S(1)}, f32[2,4,24,128]{3,2,1,0:T(8,128)S(1)}, u32[]{:S(2)}, u32[]{:S(2)}) collective-permute-start(f32[2,4,24,128]{3,2,1,0:T(8,128)S(1)} %get-tuple-element.35.p_ref), channel_id=1, source_target_pairs={{0,15},{1,2},{2,1},{3,4},{4,3},{5,6},{6,5},{7,8},{8,7},{9,10},{10,... | collective-permute-start | bytes 294920 | tf_op jit(solution)/shard_map/ppermute | solution.py:753
  22.2 0.0 collective-permute-done.5
  22.2 0.0 collective-permute-done.6
  22.2 0.0 collective-permute-done.7
  22.2 2.3 %collective-permute-done.3.pb_ref = f32[2,4,24,128]{3,2,1,0:T(8,128)S(1)} collective-permute-done((f32[2,4,24,128]{3,2,1,0:T(8,128)S(1)}, f32[2,4,24,128]{3,2,1,0:T(8,128)S(1)}, u32[]{:S(2)}, u32[]{:S(2)}) %collective-permute-start.3) | collective-permute-done | bytes 98336 | tf_op jit(solution)/shard_map/ppermute | solution.py:753
  24.4 0.0 collective-permute-done.4
  24.6 0.1 collective-permute-start.8
  24.7 0.1 multiply_select_fusion.lap_ref
  24.8 0.6 %collective-permute-start.2 = (f32[2,4,24,128]{3,2,1,0:T(8,128)S(1)}, f32[2,4,24,128]{3,2,1,0:T(8,128)S(1)}, u32[]{:S(2)}, u32[]{:S(2)}) collective-permute-start(f32[2,4,24,128]{3,2,1,0:T(8,128)S(1)} %get-tuple-element.35.p_ref), channel_id=1, source_target_pairs={{0,1},{1,0},{2,3},{3,2},{4,5},{5,4},{6,7},{7,6},{8,9},{9,8},{10,11... | collective-permute-start | bytes 294920 | tf_op jit(solution)/shard_map/ppermute | solution.py:752
  25.4 0.7 %collective-permute-done.8 = f32[8,56,128]{2,1,0:T(8,128)S(1)} collective-permute-done((f32[8,56,128]{2,1,0:T(8,128)S(1)}, f32[8,56,128]{2,1,0:T(8,128)S(1)}, u32[]{:S(2)}, u32[]{:S(2)}) %collective-permute-start.8) | collective-permute-done | bytes 229408 | tf_op jit(solution)/shard_map/ppermute | solution.py:699
  26.2 2.8 %collective-permute-start.9 = (f32[4,56,128]{2,1,0:T(8,128)S(1)}, f32[4,56,128]{2,1,0:T(8,128)S(1)}, u32[]{:S(2)}, u32[]{:S(2)}) collective-permute-start(f32[4,56,128]{2,1,0:T(8,128)S(1)} %slice_select_fusion), channel_id=1, source_target_pairs={{0,2},{1,3},{2,0},{3,1},{4,6},{5,7},{6,4},{7,5},{8,10},{9,11},{10,... | collective-permute-start | bytes 344072 | tf_op jit(solution)/shard_map/ppermute | solution.py:704
  28.9 0.0 collective-permute-done.2.pa_ref
  28.9 0.0 copy-done.5
  28.9 4.7 %shard_map.50 = (f32[4,48,16,128]{3,2,1,0:T(8,128)}, f32[48,8,128]{2,1,0:T(8,128)S(1)}, f32[2,8,128]{2,1,0:T(8,128)S(1)}, f32[48,8,128]{2,1,0:T(8,128)S(1)}) custom-call(f32[4,48,16,128]{3,2,1,0:T(8,128)S(1)} %copy-done.1, f32[4,48,16,128]{3,2,1,0:T(8,128)S(1)} %copy-done.5, bf16[48,16,128]{2,1,0:T(8,128)(2,1)S(1)} %get-tuple-element.29.disks_ref, ...), custom_call_target="tpu_custom_call" | custom-call | flops 4294967296 | bytes 1048576 | tf_op jit(solution)/shard_map/pallas_call | solution.py:756
  33.6 0.0 collective-permute-done.9
  33.7 0.1 shard_map.52
  (8 shorter events, 0.2 us)
Async XLA Ops:
  0.0 1.4 %copy-start = (f32[4,48,16,128]{3,2,1,0:T(8,128)S(1)}, f32[4,48,16,128]{3,2,1,0:T(8,128)}, u32[]{:S(2)}) copy-start(f32[4,48,16,128]{3,2,1,0:T(8,128)} %f_ref.7) | copy-start | bytes 4718596
  1.6 15.1 %collective-permute-start = (f32[48,8,128]{2,1,0:T(8,128)S(1)}, f32[48,8,128]{2,1,0:T(8,128)S(1)}, u32[]{:S(2)}, u32[]{:S(2)}) collective-permute-start(f32[48,8,128]{2,1,0:T(8,128)S(1)} %get-tuple-element.26.after_ref.sa_ref), channel_id=1, source_target_pairs={{0,16},{16,0},{32,48},{48,32},{64,80},{80,64},{96,112},{112,96},{1... | collective-permute-start | bytes 589832 | tf_op jit(solution)/shard_map/ppermute | solution.py:720
  3.0 2.6 %copy-start.2 = (f32[4,48,128]{2,1,0:T(8,128)S(1)}, f32[4,48,128]{2,1,0:T(8,128)}, u32[]{:S(2)}) copy-start(f32[4,48,128]{2,1,0:T(8,128)} %in_ref.1) | copy-start | bytes 294916
  3.0 2.6 %copy-start.3 = (s32[16]{0:T(128)S(1)}, s32[16]{0:T(128)}, u32[]{:S(2)}) copy-start(s32[16]{0:T(128)} %map_ref.1) | copy-start | bytes 196
  3.0 5.5 %copy-start.6 = (s32[100,3]{0,1:T(4,128)S(1)}, s32[100,3]{0,1:T(4,128)}, u32[]{:S(2)}) copy-start(s32[100,3]{0,1:T(4,128)} %param.6) | copy-start | bytes 3604
  3.0 5.5 %copy-start.1 = (f32[4,48,16,128]{3,2,1,0:T(8,128)S(1)}, f32[4,48,16,128]{3,2,1,0:T(8,128)}, u32[]{:S(2)}) copy-start(f32[4,48,16,128]{3,2,1,0:T(8,128)} %f_ref.7) | copy-start | bytes 4718596
  3.0 12.9 %collective-permute-start.1 = (f32[48,8,128]{2,1,0:T(8,128)S(1)}, f32[48,8,128]{2,1,0:T(8,128)S(1)}, u32[]{:S(2)}, u32[]{:S(2)}) collective-permute-start(f32[48,8,128]{2,1,0:T(8,128)S(1)} %get-tuple-element.30.sb_ref), channel_id=1, source_target_pairs={{0,1},{1,0},{2,3},{3,2},{4,5},{5,4},{6,7},{7,6},{8,9},{9,8},{10,11... | collective-permute-start | bytes 589832 | tf_op jit(solution)/shard_map/ppermute | solution.py:721
  6.5 15.7 %collective-permute-start.5 = (f32[4,56,128]{2,1,0:T(8,128)S(1)}, f32[4,56,128]{2,1,0:T(8,128)S(1)}, u32[]{:S(2)}, u32[]{:S(2)}) collective-permute-start(f32[4,56,128]{2,1,0:T(8,128)S(1)} %get-tuple-element.39), channel_id=1, source_target_pairs={{64,0},{33,1},{98,2},{115,3},{68,4},{37,5},{102,6},{119,7},{72,8},... | collective-permute-start | bytes 344072 | tf_op jit(solution)/shard_map/ppermute | solution.py:686
  7.1 15.0 %collective-permute-start.6 = (f32[4,56,128]{2,1,0:T(8,128)S(1)}, f32[4,56,128]{2,1,0:T(8,128)S(1)}, u32[]{:S(2)}, u32[]{:S(2)}) collective-permute-start(f32[4,56,128]{2,1,0:T(8,128)S(1)} %get-tuple-element.39), channel_id=1, source_target_pairs={{128,0},{145,1},{162,2},{179,3},{132,4},{149,5},{166,6},{183,7},{1... | collective-permute-start | bytes 344072 | tf_op jit(solution)/shard_map/ppermute | solution.py:686
  7.8 14.4 %collective-permute-start.7 = (f32[4,56,128]{2,1,0:T(8,128)S(1)}, f32[4,56,128]{2,1,0:T(8,128)S(1)}, u32[]{:S(2)}, u32[]{:S(2)}) collective-permute-start(f32[4,56,128]{2,1,0:T(8,128)S(1)} %get-tuple-element.39), channel_id=1, source_target_pairs={{192,0},{49,1},{226,2},{243,3},{196,4},{53,5},{230,6},{247,7},{200... | collective-permute-start | bytes 344072 | tf_op jit(solution)/shard_map/ppermute | solution.py:686
  10.4 1.1 %copy-start.4 = (f32[4,48,16,128]{3,2,1,0:T(8,128)}, f32[4,48,16,128]{3,2,1,0:T(8,128)S(1)}, u32[]{:S(2)}) copy-start(f32[4,48,16,128]{3,2,1,0:T(8,128)S(1)} %get-tuple-element.28.base_ref) | copy-start | bytes 4718596
  15.9 8.5 %collective-permute-start.4 = (f32[4,56,128]{2,1,0:T(8,128)S(1)}, f32[4,56,128]{2,1,0:T(8,128)S(1)}, u32[]{:S(2)}, u32[]{:S(2)}) collective-permute-start(f32[4,56,128]{2,1,0:T(8,128)S(1)} %get-tuple-element.39), channel_id=1, source_target_pairs={{17,1},{82,2},{211,3},{21,5},{86,6},{215,7},{25,9},{90,10},{219,11... | collective-permute-start | bytes 344072 | tf_op jit(solution)/shard_map/ppermute | solution.py:686
  17.6 11.3 %copy-start.5 = (f32[4,48,16,128]{3,2,1,0:T(8,128)S(1)}, f32[4,48,16,128]{3,2,1,0:T(8,128)}, u32[]{:S(2)}) copy-start(f32[4,48,16,128]{3,2,1,0:T(8,128)} %copy-done.4) | copy-start | bytes 4718596
  17.6 6.8 %collective-permute-start.3 = (f32[2,4,24,128]{3,2,1,0:T(8,128)S(1)}, f32[2,4,24,128]{3,2,1,0:T(8,128)S(1)}, u32[]{:S(2)}, u32[]{:S(2)}) collective-permute-start(f32[2,4,24,128]{3,2,1,0:T(8,128)S(1)} %get-tuple-element.35.p_ref), channel_id=1, source_target_pairs={{0,15},{1,2},{2,1},{3,4},{4,3},{5,6},{6,5},{7,8},{8,7},{9,10},{10,... | collective-permute-start | bytes 294920 | tf_op jit(solution)/shard_map/ppermute | solution.py:753
  24.6 1.6 %collective-permute-start.8 = (f32[8,56,128]{2,1,0:T(8,128)S(1)}, f32[8,56,128]{2,1,0:T(8,128)S(1)}, u32[]{:S(2)}, u32[]{:S(2)}) collective-permute-start(f32[8,56,128]{2,1,0:T(8,128)S(1)} %pad_maximum_fusion), channel_id=1, source_target_pairs={{0,1},{1,0},{2,3},{3,2},{4,5},{5,4},{6,7},{7,6},{8,9},{9,8},{10,11... | collective-permute-start | bytes 688136 | tf_op jit(solution)/shard_map/ppermute | solution.py:699
  24.8 4.1 %collective-permute-start.2 = (f32[2,4,24,128]{3,2,1,0:T(8,128)S(1)}, f32[2,4,24,128]{3,2,1,0:T(8,128)S(1)}, u32[]{:S(2)}, u32[]{:S(2)}) collective-permute-start(f32[2,4,24,128]{3,2,1,0:T(8,128)S(1)} %get-tuple-element.35.p_ref), channel_id=1, source_target_pairs={{0,1},{1,0},{2,3},{3,2},{4,5},{5,4},{6,7},{7,6},{8,9},{9,8},{10,11... | collective-permute-start | bytes 294920 | tf_op jit(solution)/shard_map/ppermute | solution.py:752
  26.2 7.5 %collective-permute-start.9 = (f32[4,56,128]{2,1,0:T(8,128)S(1)}, f32[4,56,128]{2,1,0:T(8,128)S(1)}, u32[]{:S(2)}, u32[]{:S(2)}) collective-permute-start(f32[4,56,128]{2,1,0:T(8,128)S(1)} %slice_select_fusion), channel_id=1, source_target_pairs={{0,2},{1,3},{2,0},{3,1},{4,6},{5,7},{6,4},{7,5},{8,10},{9,11},{10,... | collective-permute-start | bytes 344072 | tf_op jit(solution)/shard_map/ppermute | solution.py:704

commit v2 on v1

--- a/solution.py
+++ b/solution.py
@@ -18,7 +18,7 @@
 FAR = -100000
 F32 = jnp.float32
 UNROLL = 16
-WIDE = 24
+WIDE = 48
 TRADES = ((2, 5), (3, 13))
 CHUNK = 8
 GROUP = 4
@@ -165,7 +165,7 @@
             p_ref[half, i, 0:16, :] = packed[i]
 
 
-def base_kernel(f_ref, fp_ref, base_ref, disks_ref, sums_ref, rows_ref):
+def base_kernel(f_ref, fp_ref, base_ref, disks_ref, masks_ref, sums_ref, rows_ref):
     nz = f_ref.shape[1]
     first_x = lax.axis_index("gx") * 16
     first_y = lax.axis_index("gy") * 128
@@ -216,6 +216,24 @@
     sums_ref[0:1, :] = jnp.sum(acc[0] * mask_x, axis=0, keepdims=True)
     sums_ref[1:2, :] = jnp.sum(acc[1] * mask_x, axis=0, keepdims=True)
     sums_ref[2:8, :] = jnp.zeros((6, 128), F32)
+
+    fy, fz = fp[1:2], fp[2:3]
+    all_y = lax.axis_size("gy") * 128
+    at = iota((256, 128), 0)
+    level = at // 4
+    k_at = at % 4
+    mask_level = within(level, fz, DISK_Z) * (level < nz).astype(F32)
+    y_left = jnp.where(k_at == 1, jnp.where(first_y == 0, all_y - 1, first_y - 1), first_y)
+    y_right = jnp.where(
+        k_at == 1, first_y + 127, jnp.where(first_y + 128 == all_y, 0, first_y + 128)
+    )
+    middle = ((k_at == 1) | (k_at == 2)).astype(F32)
+    mask_left = mask_level * within(y_left, fy, DISK_Y) * middle
+    mask_right = mask_level * within(y_right, fy, DISK_Y) * middle
+    y_cols = jnp.where(k_at == 1, y_left, y_right)
+    mask_cols = mask_level * within(y_cols, fy, DISK_Y) * middle
+    for i, mask in enumerate((mask_left, mask_right, mask_cols)):
+        masks_ref[i] = mask.astype(jnp.bfloat16)
 
 
 def rim_kernel(
@@ -332,6 +350,7 @@
     f_ref,
     base_ref,
     disks_ref,
+    masks_ref,
     cur_ref,
     west_ref,
     east_ref,
@@ -357,7 +376,6 @@
     tile_x = lax.axis_index("gx")
     tile_y = lax.axis_index("gy")
     last_x = lax.axis_size("gx") - 1
-    all_y = lax.axis_size("gy") * 128
     even_y = tile_y % 2 == 0
     first_x = tile_x * 16
     first_y = tile_y * 128
@@ -394,17 +412,6 @@
         return -GAIN * DT * speed * jnp.abs(speed)
 
     thrust1 = thrust_of(total(0))
-    at = iota((256, 128), 0)
-    level = at // 4
-    k_at = at % 4
-    mask_level = within(level, fz, DISK_Z) * (level < nz).astype(F32)
-    y_left = jnp.where(k_at == 1, jnp.where(first_y == 0, all_y - 1, first_y - 1), first_y)
-    y_right = jnp.where(
-        k_at == 1, first_y + 127, jnp.where(first_y + 128 == all_y, 0, first_y + 128)
-    )
-    middle = ((k_at == 1) | (k_at == 2)).astype(F32)
-    mask_left = mask_level * within(y_left, fy, DISK_Y) * middle
-    mask_right = mask_level * within(y_right, fy, DISK_Y) * middle
     k256 = iota((24, 256), 1) % 4
 
     def facing(cols, mask):
@@ -412,9 +419,9 @@
         cs, cn = upwind(v)
         term = jnp.where(k256 == 1, cn * pltpu.roll(u, 255, 1), cs * pltpu.roll(u, 1, 1))
         term = jnp.concatenate([term, jnp.zeros((8, 256), F32)], axis=0)
-        return dot_nn(term, mask.astype(jnp.bfloat16))
-
-    faces = facing(left_cols, mask_left) + facing(right_cols, mask_right)
+        return dot_nn(term, mask)
+
+    faces = facing(left_cols, masks_ref[0]) + facing(right_cols, masks_ref[1])
     sub32 = iota((32, 128), 0)
     column = jnp.where(sub32 == 16, -1, jnp.where(sub32 == 17, 16, sub32))
     mask_x32 = within(first_x + column, fx, DISK_X) * (sub32 < 18).astype(F32)
@@ -445,9 +452,7 @@
         weights = span * (thrust1 * within(first_x + x, fx, DISK_X))
         rim_force_ref[side] = dot_disks(levels, weights)
     by_x1 = within(first_x + sub, fx, DISK_X) * thrust1
-    y_cols = jnp.where(k_at == 1, y_left, y_right)
-    mask_cols = mask_level * within(y_cols, fy, DISK_Y) * middle
-    force_cols = dot_nt(by_x1, mask_cols.astype(jnp.bfloat16))
+    force_cols = dot_nt(by_x1, masks_ref[2])
 
     lane256 = iota((16, 256), 1)
     sub256 = iota((16, 256), 0)
@@ -734,11 +739,12 @@
         (shape(4, levels + 8, 128), jax.ShapeDtypeStruct((GROUP, levels + 8, 128), jnp.int32)),
         ins=[SMEM, VMEM, VMEM],
     )(block_map, inflow, own)
-    base, disks, sums = call(
+    base, disks, masks, sums = call(
         base_kernel,
         (
             shape(*flow_state.shape),
             jax.ShapeDtypeStruct((levels, 16, 128), jnp.bfloat16),
+            jax.ShapeDtypeStruct((3, 256, 128), jnp.bfloat16),
             shape(8, 128),
         ),
         [pltpu.VMEM((2, levels, 16, 128), F32)],
@@ -768,7 +774,7 @@
         ],
         outs=[ANY, VMEM, VMEM, VMEM],
         flops=STEPS_COST,
-    )(flow_state, base, disks, near, west, east, own, side_a, side_b, fp, lap)
+    )(flow_state, base, disks, masks, near, west, east, own, side_a, side_b, fp, lap)
     return call(
         fix_kernel,
         shape(*flow_state.shape),

time: 34 us -> 33.4 us (0.982)
  the two profiles are of different devices: /device:TPU:161 before, /device:TPU:128 now
where the time goes in v2:
time: 33.4 us; the launch traced here: 33.2 us
  waiting for transfers between devices  13.8 us (41%)
  Pallas kernels  7.73 us (23%)
  starting transfers between devices  7.61 us (23%)
  local copies, waits for them, and re-layouts  3.37 us (10%)
  other arithmetic  0.42 us (1%)
    ppermute x1, waiting for transfers between devices, body(): recv_b = lax.ppermute(send_b, ('gx', 'gy'), pairs_inside(count_x, count_y))  6.52 us
    ppermute x1, waiting for transfers between devices, body(): side_b = lax.ppermute(own, 'gy', pairs(count_y, True))  4.89 us
    pallas_call x1, Pallas kernels, body(): call(steps_kernel, (shape(*flow_state.shape), x_pack, shape(2, 8, 128), x...  3.5 us
    ppermute x4, starting transfers between devices, send_inlet(): heard[m] = lax.ppermute(sent, ('gx', 'gy'), moves)  3.29 us
    unnamed x14, local copies, waits for them, and re-layouts  2.57 us
    ppermute x1, starting transfers between devices, body(): recv_a = lax.ppermute(send_a, 'gx', pairs(count_x, False))  1.66 us
    pallas_call x1, Pallas kernels, body(): call(base_kernel, (shape(*flow_state.shape), jax.ShapeDtypeStruct((levels...  1.65 us
    ppermute x1, waiting for transfers between devices, share_inlet(): other = lax.ppermute(theirs, 'gy', [(j, j ^ 2) for j in range(count_y)])  1.61 us
  transfers between devices with their start and end apart: 10, of which 5 were waited for; matrix products, arithmetic and copies ran while one was open for 3% of the time, Pallas kernels for 22%

profile of v2, /device:TPU:128, one launch (start us, length us, event | category | flops | bytes accessed | tf_op | source)
XLA Modules:
  0.0 33.2 jit_solution(14491689927054328020)
XLA Ops:
  0.0 0.0 copy-start
  0.0 1.4 %copy-done = f32[4,48,16,128]{3,2,1,0:T(8,128)S(1)} copy-done((f32[4,48,16,128]{3,2,1,0:T(8,128)S(1)}, f32[4,48,16,128]{3,2,1,0:T(8,128)}, u32[]{:S(2)}) %copy-start) | copy-done | bytes 1572888
  1.4 0.2 shard_map.46
  1.6 1.7 %collective-permute-start = (f32[48,8,128]{2,1,0:T(8,128)S(1)}, f32[48,8,128]{2,1,0:T(8,128)S(1)}, u32[]{:S(2)}, u32[]{:S(2)}) collective-permute-start(f32[48,8,128]{2,1,0:T(8,128)S(1)} %get-tuple-element.27.after_ref.sa_ref), channel_id=1, source_target_pairs={{0,16},{16,0},{32,48},{48,32},{64,80},{80,64},{96,112},{112,96},{1... | collective-permute-start | bytes 589832 | tf_op jit(solution)/shard_map/ppermute | solution.py:725
  3.3 0.0 copy-start.2
  3.3 0.0 copy-start.3
  3.3 0.0 copy-start.6
  3.3 0.0 copy-start.1
  3.3 1.4 %collective-permute-start.1 = (f32[48,8,128]{2,1,0:T(8,128)S(1)}, f32[48,8,128]{2,1,0:T(8,128)S(1)}, u32[]{:S(2)}, u32[]{:S(2)}) collective-permute-start(f32[48,8,128]{2,1,0:T(8,128)S(1)} %get-tuple-element.32.sb_ref), channel_id=1, source_target_pairs={{0,1},{1,0},{2,3},{3,2},{4,5},{5,4},{6,7},{7,6},{8,9},{9,8},{10,11... | collective-permute-start | bytes 589832 | tf_op jit(solution)/shard_map/ppermute | solution.py:726
  4.7 0.6 %shard_map.48.p_in.after_ref = f32[2,4,24,128]{3,2,1,0:T(8,128)S(1)} custom-call(f32[4,48,16,128]{3,2,1,0:T(8,128)S(1)} %copy-done, f32[48,8,128]{2,1,0:T(8,128)S(1)} %get-tuple-element.27.after_ref.sa_ref), custom_call_target="tpu_custom_call" | custom-call | flops 8589934592 | bytes 1048576 | tf_op jit(solution)/shard_map/pallas_call | solution.py:736
  5.3 0.0 copy-done.2
  5.3 0.0 copy-done.3
  5.3 0.8 %shard_map.51 = (f32[4,56,128]{2,1,0:T(8,128)S(1)}, s32[4,56,128]{2,1,0:T(8,128)S(1)}) custom-call(s32[16]{0:T(128)S(1)} %copy-done.3, f32[4,48,128]{2,1,0:T(8,128)S(1)} %copy-done.2, f32[2,4,24,128]{3,2,1,0:T(8,128)S(1)} %shard_map.48.p_in.after_ref), custom_call_target="tpu_custom_call" | custom-call | flops 1048576 | bytes 1048576 | tf_op jit(solution)/shard_map/pallas_call | solution.py:737
  6.1 0.7 %collective-permute-start.5 = (f32[4,56,128]{2,1,0:T(8,128)S(1)}, f32[4,56,128]{2,1,0:T(8,128)S(1)}, u32[]{:S(2)}, u32[]{:S(2)}) collective-permute-start(f32[4,56,128]{2,1,0:T(8,128)S(1)} %get-tuple-element.41), channel_id=1, source_target_pairs={{64,0},{33,1},{98,2},{115,3},{68,4},{37,5},{102,6},{119,7},{72,8},... | collective-permute-start | bytes 344072 | tf_op jit(solution)/shard_map/ppermute | solution.py:691
  6.8 1.3 %collective-permute-start.6 = (f32[4,56,128]{2,1,0:T(8,128)S(1)}, f32[4,56,128]{2,1,0:T(8,128)S(1)}, u32[]{:S(2)}, u32[]{:S(2)}) collective-permute-start(f32[4,56,128]{2,1,0:T(8,128)S(1)} %get-tuple-element.41), channel_id=1, source_target_pairs={{128,0},{145,1},{162,2},{179,3},{132,4},{149,5},{166,6},{183,7},{1... | collective-permute-start | bytes 344072 | tf_op jit(solution)/shard_map/ppermute | solution.py:691
  8.1 0.7 %collective-permute-start.7 = (f32[4,56,128]{2,1,0:T(8,128)S(1)}, f32[4,56,128]{2,1,0:T(8,128)S(1)}, u32[]{:S(2)}, u32[]{:S(2)}) collective-permute-start(f32[4,56,128]{2,1,0:T(8,128)S(1)} %get-tuple-element.41), channel_id=1, source_target_pairs={{192,0},{49,1},{226,2},{243,3},{196,4},{53,5},{230,6},{247,7},{200... | collective-permute-start | bytes 344072 | tf_op jit(solution)/shard_map/ppermute | solution.py:691
  8.8 0.0 copy-done.6
  8.8 0.0 copy-done.1
  8.8 1.7 %shard_map.47 = (f32[4,48,16,128]{3,2,1,0:T(8,128)S(1)}, bf16[48,16,128]{2,1,0:T(8,128)(2,1)S(1)}, bf16[3,256,128]{2,1,0:T(8,128)(2,1)S(1)}, f32[8,128]{1,0:T(8,128)S(1)}) custom-call(f32[4,48,16,128]{3,2,1,0:T(8,128)S(1)} %copy-done.1, s32[8,128]{1,0:T(8,128)S(1)} %pad.4.fp_ref), custom_call_target="tpu_custom_call" | custom-call | flops 1048576 | bytes 1048576 | tf_op jit(solution)/shard_map/pallas_call | solution.py:742
  10.5 0.0 copy-start.4
  10.5 1.1 %copy-done.4 = f32[4,48,16,128]{3,2,1,0:T(8,128)} copy-done((f32[4,48,16,128]{3,2,1,0:T(8,128)}, f32[4,48,16,128]{3,2,1,0:T(8,128)S(1)}, u32[]{:S(2)}) %copy-start.4) | copy-done | bytes 1572888
  11.6 6.5 %collective-permute-done.1.rb_ref = f32[48,8,128]{2,1,0:T(8,128)S(1)} collective-permute-done((f32[48,8,128]{2,1,0:T(8,128)S(1)}, f32[48,8,128]{2,1,0:T(8,128)S(1)}, u32[]{:S(2)}, u32[]{:S(2)}) %collective-permute-start.1) | collective-permute-done | bytes 196640 | tf_op jit(solution)/shard_map/ppermute | solution.py:726
  18.1 0.7 %collective-permute-start.4 = (f32[4,56,128]{2,1,0:T(8,128)S(1)}, f32[4,56,128]{2,1,0:T(8,128)S(1)}, u32[]{:S(2)}, u32[]{:S(2)}) collective-permute-start(f32[4,56,128]{2,1,0:T(8,128)S(1)} %get-tuple-element.41), channel_id=1, source_target_pairs={{17,1},{82,2},{211,3},{21,5},{86,6},{215,7},{25,9},{90,10},{219,11... | collective-permute-start | bytes 344072 | tf_op jit(solution)/shard_map/ppermute | solution.py:691
  18.8 0.1 fusion.1
  18.9 0.0 collective-permute-done.ra_ref
  18.9 0.9 %shard_map.49 = (f32[2,4,24,128]{3,2,1,0:T(8,128)S(1)}, f32[48,8,128]{2,1,0:T(8,128)S(1)}, f32[48,8,128]{2,1,0:T(8,128)S(1)}, f32[48,8,128]{2,1,0:T(8,128)S(1)}) custom-call(f32[48,8,128]{2,1,0:T(8,128)S(1)} %get-tuple-element.27.after_ref.sa_ref, f32[48,8,128]{2,1,0:T(8,128)S(1)} %get-tuple-element.32.sb_ref, ...), custom_call_target="tpu_custom_call" | custom-call | flops 1048576 | bytes 1048576 | tf_op jit(solution)/shard_map/pallas_call | solution.py:755
  19.8 0.0 copy-start.5
  19.8 0.5 %collective-permute-start.3 = (f32[2,4,24,128]{3,2,1,0:T(8,128)S(1)}, f32[2,4,24,128]{3,2,1,0:T(8,128)S(1)}, u32[]{:S(2)}, u32[]{:S(2)}) collective-permute-start(f32[2,4,24,128]{3,2,1,0:T(8,128)S(1)} %get-tuple-element.37.p_ref), channel_id=1, source_target_pairs={{0,15},{1,2},{2,1},{3,4},{4,3},{5,6},{6,5},{7,8},{8,7},{9,10},{10,... | collective-permute-start | bytes 294920 | tf_op jit(solution)/shard_map/ppermute | solution.py:759
  20.3 0.8 %fusion.4 = (s32[128]{0:T(128)S(1)}, s32[128]{0:T(128)S(1)}, s32[128]{0:T(128)S(1)}) fusion(s32[3,100]{1,0:T(4,128)} %bitcast.37), kind=kLoop, calls=%fused_computation.32 | loop fusion | bytes 2736 | tf_op jit(solution)/shard_map/sub | solution.py:732
  21.1 0.0 collective-permute-done.5
  21.1 0.0 collective-permute-done.6
  21.1 0.0 collective-permute-done.7
  21.2 4.9 %collective-permute-done.3.pb_ref = f32[2,4,24,128]{3,2,1,0:T(8,128)S(1)} collective-permute-done((f32[2,4,24,128]{3,2,1,0:T(8,128)S(1)}, f32[2,4,24,128]{3,2,1,0:T(8,128)S(1)}, u32[]{:S(2)}, u32[]{:S(2)}) %collective-permute-start.3) | collective-permute-done | bytes 98336 | tf_op jit(solution)/shard_map/ppermute | solution.py:759
  26.0 0.0 collective-permute-done.4
  26.2 0.1 collective-permute-start.8
  26.3 0.1 multiply_select_fusion.lap_ref
  26.4 0.6 %collective-permute-start.2 = (f32[2,4,24,128]{3,2,1,0:T(8,128)S(1)}, f32[2,4,24,128]{3,2,1,0:T(8,128)S(1)}, u32[]{:S(2)}, u32[]{:S(2)}) collective-permute-start(f32[2,4,24,128]{3,2,1,0:T(8,128)S(1)} %get-tuple-element.37.p_ref), channel_id=1, source_target_pairs={{0,1},{1,0},{2,3},{3,2},{4,5},{5,4},{6,7},{7,6},{8,9},{9,8},{10,11... | collective-permute-start | bytes 294920 | tf_op jit(solution)/shard_map/ppermute | solution.py:758
  27.0 0.7 %collective-permute-done.8 = f32[8,56,128]{2,1,0:T(8,128)S(1)} collective-permute-done((f32[8,56,128]{2,1,0:T(8,128)S(1)}, f32[8,56,128]{2,1,0:T(8,128)S(1)}, u32[]{:S(2)}, u32[]{:S(2)}) %collective-permute-start.8) | collective-permute-done | bytes 229408 | tf_op jit(solution)/shard_map/ppermute | solution.py:704
  27.8 0.1 collective-permute-start.9
  27.9 0.1 collective-permute-done.2.pa_ref
  27.9 0.0 copy-done.5
  27.9 3.5 %shard_map.50 = (f32[4,48,16,128]{3,2,1,0:T(8,128)}, f32[48,8,128]{2,1,0:T(8,128)S(1)}, f32[2,8,128]{2,1,0:T(8,128)S(1)}, f32[48,8,128]{2,1,0:T(8,128)S(1)}) custom-call(f32[4,48,16,128]{3,2,1,0:T(8,128)S(1)} %copy-done.1, f32[4,48,16,128]{3,2,1,0:T(8,128)S(1)} %copy-done.5, bf16[48,16,128]{2,1,0:T(8,128)(2,1)S(1)} %get-tuple-element.30.disks_ref, ...), custom_call_target="tpu_custom_call" | custom-call | flops 4294967296 | bytes 1048576 | tf_op jit(solution)/shard_map/pallas_call | solution.py:762
  31.5 1.6 %collective-permute-done.9 = f32[4,56,128]{2,1,0:T(8,128)S(1)} collective-permute-done((f32[4,56,128]{2,1,0:T(8,128)S(1)}, f32[4,56,128]{2,1,0:T(8,128)S(1)}, u32[]{:S(2)}, u32[]{:S(2)}) %collective-permute-start.9) | collective-permute-done | bytes 114720 | tf_op jit(solution)/shard_map/ppermute | solution.py:709
  33.1 0.1 fusion.in_ref
  33.1 0.1 shard_map.52
  (6 shorter events, 0.2 us)
Async XLA Ops:
  0.0 1.4 %copy-start = (f32[4,48,16,128]{3,2,1,0:T(8,128)S(1)}, f32[4,48,16,128]{3,2,1,0:T(8,128)}, u32[]{:S(2)}) copy-start(f32[4,48,16,128]{3,2,1,0:T(8,128)} %f_ref.7) | copy-start | bytes 4718596
  1.6 17.3 %collective-permute-start = (f32[48,8,128]{2,1,0:T(8,128)S(1)}, f32[48,8,128]{2,1,0:T(8,128)S(1)}, u32[]{:S(2)}, u32[]{:S(2)}) collective-permute-start(f32[48,8,128]{2,1,0:T(8,128)S(1)} %get-tuple-element.27.after_ref.sa_ref), channel_id=1, source_target_pairs={{0,16},{16,0},{32,48},{48,32},{64,80},{80,64},{96,112},{112,96},{1... | collective-permute-start | bytes 589832 | tf_op jit(solution)/shard_map/ppermute | solution.py:725
  3.3 2.0 %copy-start.2 = (f32[4,48,128]{2,1,0:T(8,128)S(1)}, f32[4,48,128]{2,1,0:T(8,128)}, u32[]{:S(2)}) copy-start(f32[4,48,128]{2,1,0:T(8,128)} %in_ref.1) | copy-start | bytes 294916
  3.3 2.0 %copy-start.3 = (s32[16]{0:T(128)S(1)}, s32[16]{0:T(128)}, u32[]{:S(2)}) copy-start(s32[16]{0:T(128)} %map_ref.1) | copy-start | bytes 196
  3.3 5.5 %copy-start.6 = (s32[100,3]{0,1:T(4,128)S(1)}, s32[100,3]{0,1:T(4,128)}, u32[]{:S(2)}) copy-start(s32[100,3]{0,1:T(4,128)} %param.6) | copy-start | bytes 3604
  3.3 5.5 %copy-start.1 = (f32[4,48,16,128]{3,2,1,0:T(8,128)S(1)}, f32[4,48,16,128]{3,2,1,0:T(8,128)}, u32[]{:S(2)}) copy-start(f32[4,48,16,128]{3,2,1,0:T(8,128)} %f_ref.7) | copy-start | bytes 4718596
  3.3 14.8 %collective-permute-start.1 = (f32[48,8,128]{2,1,0:T(8,128)S(1)}, f32[48,8,128]{2,1,0:T(8,128)S(1)}, u32[]{:S(2)}, u32[]{:S(2)}) collective-permute-start(f32[48,8,128]{2,1,0:T(8,128)S(1)} %get-tuple-element.32.sb_ref), channel_id=1, source_target_pairs={{0,1},{1,0},{2,3},{3,2},{4,5},{5,4},{6,7},{7,6},{8,9},{9,8},{10,11... | collective-permute-start | bytes 589832 | tf_op jit(solution)/shard_map/ppermute | solution.py:726
  6.1 15.0 %collective-permute-start.5 = (f32[4,56,128]{2,1,0:T(8,128)S(1)}, f32[4,56,128]{2,1,0:T(8,128)S(1)}, u32[]{:S(2)}, u32[]{:S(2)}) collective-permute-start(f32[4,56,128]{2,1,0:T(8,128)S(1)} %get-tuple-element.41), channel_id=1, source_target_pairs={{64,0},{33,1},{98,2},{115,3},{68,4},{37,5},{102,6},{119,7},{72,8},... | collective-permute-start | bytes 344072 | tf_op jit(solution)/shard_map/ppermute | solution.py:691
  6.8 14.3 %collective-permute-start.6 = (f32[4,56,128]{2,1,0:T(8,128)S(1)}, f32[4,56,128]{2,1,0:T(8,128)S(1)}, u32[]{:S(2)}, u32[]{:S(2)}) collective-permute-start(f32[4,56,128]{2,1,0:T(8,128)S(1)} %get-tuple-element.41), channel_id=1, source_target_pairs={{128,0},{145,1},{162,2},{179,3},{132,4},{149,5},{166,6},{183,7},{1... | collective-permute-start | bytes 344072 | tf_op jit(solution)/shard_map/ppermute | solution.py:691
  8.1 13.0 %collective-permute-start.7 = (f32[4,56,128]{2,1,0:T(8,128)S(1)}, f32[4,56,128]{2,1,0:T(8,128)S(1)}, u32[]{:S(2)}, u32[]{:S(2)}) collective-permute-start(f32[4,56,128]{2,1,0:T(8,128)S(1)} %get-tuple-element.41), channel_id=1, source_target_pairs={{192,0},{49,1},{226,2},{243,3},{196,4},{53,5},{230,6},{247,7},{200... | collective-permute-start | bytes 344072 | tf_op jit(solution)/shard_map/ppermute | solution.py:691
  10.5 1.1 %copy-start.4 = (f32[4,48,16,128]{3,2,1,0:T(8,128)}, f32[4,48,16,128]{3,2,1,0:T(8,128)S(1)}, u32[]{:S(2)}) copy-start(f32[4,48,16,128]{3,2,1,0:T(8,128)S(1)} %get-tuple-element.29.base_ref) | copy-start | bytes 4718596
  18.1 7.9 %collective-permute-start.4 = (f32[4,56,128]{2,1,0:T(8,128)S(1)}, f32[4,56,128]{2,1,0:T(8,128)S(1)}, u32[]{:S(2)}, u32[]{:S(2)}) collective-permute-start(f32[4,56,128]{2,1,0:T(8,128)S(1)} %get-tuple-element.41), channel_id=1, source_target_pairs={{17,1},{82,2},{211,3},{21,5},{86,6},{215,7},{25,9},{90,10},{219,11... | collective-permute-start | bytes 344072 | tf_op jit(solution)/shard_map/ppermute | solution.py:691
  19.8 8.2 %copy-start.5 = (f32[4,48,16,128]{3,2,1,0:T(8,128)S(1)}, f32[4,48,16,128]{3,2,1,0:T(8,128)}, u32[]{:S(2)}) copy-start(f32[4,48,16,128]{3,2,1,0:T(8,128)} %copy-done.4) | copy-start | bytes 4718596
  19.8 6.2 %collective-permute-start.3 = (f32[2,4,24,128]{3,2,1,0:T(8,128)S(1)}, f32[2,4,24,128]{3,2,1,0:T(8,128)S(1)}, u32[]{:S(2)}, u32[]{:S(2)}) collective-permute-start(f32[2,4,24,128]{3,2,1,0:T(8,128)S(1)} %get-tuple-element.37.p_ref), channel_id=1, source_target_pairs={{0,15},{1,2},{2,1},{3,4},{4,3},{5,6},{6,5},{7,8},{8,7},{9,10},{10,... | collective-permute-start | bytes 294920 | tf_op jit(solution)/shard_map/ppermute | solution.py:759
  26.2 1.6 %collective-permute-start.8 = (f32[8,56,128]{2,1,0:T(8,128)S(1)}, f32[8,56,128]{2,1,0:T(8,128)S(1)}, u32[]{:S(2)}, u32[]{:S(2)}) collective-permute-start(f32[8,56,128]{2,1,0:T(8,128)S(1)} %pad_maximum_fusion), channel_id=1, source_target_pairs={{0,1},{1,0},{2,3},{3,2},{4,5},{5,4},{6,7},{7,6},{8,9},{9,8},{10,11... | collective-permute-start | bytes 688136 | tf_op jit(solution)/shard_map/ppermute | solution.py:704
  26.4 1.5 %collective-permute-start.2 = (f32[2,4,24,128]{3,2,1,0:T(8,128)S(1)}, f32[2,4,24,128]{3,2,1,0:T(8,128)S(1)}, u32[]{:S(2)}, u32[]{:S(2)}) collective-permute-start(f32[2,4,24,128]{3,2,1,0:T(8,128)S(1)} %get-tuple-element.37.p_ref), channel_id=1, source_target_pairs={{0,1},{1,0},{2,3},{3,2},{4,5},{5,4},{6,7},{7,6},{8,9},{9,8},{10,11... | collective-permute-start | bytes 294920 | tf_op jit(solution)/shard_map/ppermute | solution.py:758
  27.8 5.3 %collective-permute-start.9 = (f32[4,56,128]{2,1,0:T(8,128)S(1)}, f32[4,56,128]{2,1,0:T(8,128)S(1)}, u32[]{:S(2)}, u32[]{:S(2)}) collective-permute-start(f32[4,56,128]{2,1,0:T(8,128)S(1)} %slice_select_fusion), channel_id=1, source_target_pairs={{0,2},{1,3},{2,0},{3,1},{4,6},{5,7},{6,4},{7,5},{8,10},{9,11},{10,... | collective-permute-start | bytes 344072 | tf_op jit(solution)/shard_map/ppermute | solution.py:709

commit v3 on v2

--- a/solution.py
+++ b/solution.py
@@ -692,7 +692,7 @@
     return [heard[m] for m in range(4)]
 
 
-def share_inlet(msg, heard, code, count_y):
+def share_inlet(own, msg, heard, code, count_y):
     heard[0] = jnp.where(lax.axis_index("gy") % GROUP == 0, msg, heard[0])
 
     def pick(k):
@@ -701,13 +701,14 @@
             out = jnp.where(code[k] & 7 == m, heard[m], out)
         return out
 
-    core = lax.ppermute(
-        jnp.concatenate([pick(1), pick(3)]), "gy", [(j, j ^ 1) for j in range(count_y)]
-    )
+    parts = [x.reshape(-1, 128) for x in (own, pick(1), pick(3))]
+    got = lax.ppermute(jnp.concatenate(parts), "gy", pairs(count_y, False))
+    side = got[: parts[0].shape[0]].reshape(own.shape)
+    core = got[parts[0].shape[0] :].reshape(8, *msg.shape[1:])
     mine = jnp.where(code[0] & 8 != 0, pick(0), core[0:4])
     theirs = jnp.where(code[2] & 8 != 0, pick(2), core[4:8])
     other = lax.ppermute(theirs, "gy", [(j, j ^ 2) for j in range(count_y)])
-    return jnp.where(code[0] & 16 != 0, mine, other)
+    return side, jnp.where(code[0] & 16 != 0, mine, other)
 
 
 def body(flow_state, inflow, footprint, block_map):
@@ -755,10 +756,9 @@
     own, near, west, east = call(
         rim_kernel, (y_pack, x_pack, x_pack, x_pack), [pltpu.VMEM((levels, 8, 128), F32)] * 3
     )(send_a, send_b, recv_a, recv_b, fp, sums, own)
-    side_a = lax.ppermute(own, "gy", pairs(count_y, False))
     side_b = lax.ppermute(own, "gy", pairs(count_y, True))
     *heard, _ = lax.optimization_barrier((*heard, side_b))
-    inlet = share_inlet(msg, list(heard), code, count_y)
+    side_a, inlet = share_inlet(own, msg, list(heard), code, count_y)
     out, first, corner, last = call(
         steps_kernel,
         (shape(*flow_state.shape), x_pack, shape(2, 8, 128), x_pack),

time: 33.4 us -> 33.5 us (level)
  waiting for transfers between devices: 13.8 us -> 14.6 us
  starting transfers between devices: 7.61 us -> 7.03 us
    ppermute x2 -> x1, waiting for transfers between devices: 0.8 us -> 1.46 us  [share_inlet(): got = lax.ppermute(jnp.concatenate(parts), 'gy', pairs(count_y, False))]
    ppermute x2 -> x1, starting transfers between devices: 0.67 us -> 0.09 us  [share_inlet(): got = lax.ppermute(jnp.concatenate(parts), 'gy', pairs(count_y, False))]
  transfers between devices with their start and end apart: 10 -> 9, of which waited for: 5 -> 4; matrix products, arithmetic and copies ran while one was open for 3% -> 3% of each run, Pallas kernels for 22% -> 22%
where the time goes in v3:
time: 33.5 us; the launch traced here: 33.3 us
  waiting for transfers between devices  14.6 us (44%)
  Pallas kernels  7.6 us (23%)
  starting transfers between devices  7.03 us (21%)
  local copies, waits for them, and re-layouts  3.39 us (10%)
  other arithmetic  0.39 us (1%)
    ppermute x1, waiting for transfers between devices, body(): recv_b = lax.ppermute(send_b, ('gx', 'gy'), pairs_inside(count_x, count_y))  6.52 us
    ppermute x1, waiting for transfers between devices, body(): side_b = lax.ppermute(own, 'gy', pairs(count_y, True))  4.89 us
    pallas_call x1, Pallas kernels, body(): call(steps_kernel, (shape(*flow_state.shape), x_pack, shape(2, 8, 128), x...  3.39 us
    ppermute x4, starting transfers between devices, send_inlet(): heard[m] = lax.ppermute(sent, ('gx', 'gy'), moves)  3.29 us
    unnamed x14, local copies, waits for them, and re-layouts  2.56 us
    ppermute x1, waiting for transfers between devices, share_inlet(): other = lax.ppermute(theirs, 'gy', [(j, j ^ 2) for j in range(count_y)])  1.75 us
    ppermute x1, starting transfers between devices, body(): recv_a = lax.ppermute(send_a, 'gx', pairs(count_x, False))  1.66 us
    pallas_call x1, Pallas kernels, body(): call(base_kernel, (shape(*flow_state.shape), jax.ShapeDtypeStruct((levels...  1.66 us
  transfers between devices with their start and end apart: 9, of which 4 were waited for; matrix products, arithmetic and copies ran while one was open for 3% of the time, Pallas kernels for 22%

profile of v3, /device:TPU:128, one launch (start us, length us, event | category | flops | bytes accessed | tf_op | source)
XLA Modules:
  0.0 33.3 jit_solution(10719177504514006906)
XLA Ops:
  0.0 0.0 copy-start
  0.0 1.4 %copy-done = f32[4,48,16,128]{3,2,1,0:T(8,128)S(1)} copy-done((f32[4,48,16,128]{3,2,1,0:T(8,128)S(1)}, f32[4,48,16,128]{3,2,1,0:T(8,128)}, u32[]{:S(2)}) %copy-start) | copy-done | bytes 1572888
  1.4 0.2 shard_map.46
  1.6 1.7 %collective-permute-start = (f32[48,8,128]{2,1,0:T(8,128)S(1)}, f32[48,8,128]{2,1,0:T(8,128)S(1)}, u32[]{:S(2)}, u32[]{:S(2)}) collective-permute-start(f32[48,8,128]{2,1,0:T(8,128)S(1)} %get-tuple-element.27.after_ref.sa_ref), channel_id=1, source_target_pairs={{0,16},{16,0},{32,48},{48,32},{64,80},{80,64},{96,112},{112,96},{1... | collective-permute-start | bytes 589832 | tf_op jit(solution)/shard_map/ppermute | solution.py:726
  3.3 0.0 copy-start.2
  3.3 0.0 copy-start.3
  3.3 0.0 copy-start.6
  3.3 0.0 copy-start.1
  3.3 1.4 %collective-permute-start.1 = (f32[48,8,128]{2,1,0:T(8,128)S(1)}, f32[48,8,128]{2,1,0:T(8,128)S(1)}, u32[]{:S(2)}, u32[]{:S(2)}) collective-permute-start(f32[48,8,128]{2,1,0:T(8,128)S(1)} %get-tuple-element.32.sb_ref), channel_id=1, source_target_pairs={{0,1},{1,0},{2,3},{3,2},{4,5},{5,4},{6,7},{7,6},{8,9},{9,8},{10,11... | collective-permute-start | bytes 589832 | tf_op jit(solution)/shard_map/ppermute | solution.py:727
  4.7 0.6 %shard_map.48.p_in.after_ref = f32[2,4,24,128]{3,2,1,0:T(8,128)S(1)} custom-call(f32[4,48,16,128]{3,2,1,0:T(8,128)S(1)} %copy-done, f32[48,8,128]{2,1,0:T(8,128)S(1)} %get-tuple-element.27.after_ref.sa_ref), custom_call_target="tpu_custom_call" | custom-call | flops 8589934592 | bytes 1048576 | tf_op jit(solution)/shard_map/pallas_call | solution.py:737
  5.3 0.0 copy-done.2
  5.3 0.0 copy-done.3
  5.3 0.8 %shard_map.50 = (f32[4,56,128]{2,1,0:T(8,128)S(1)}, s32[4,56,128]{2,1,0:T(8,128)S(1)}) custom-call(s32[16]{0:T(128)S(1)} %copy-done.3, f32[4,48,128]{2,1,0:T(8,128)S(1)} %copy-done.2, f32[2,4,24,128]{3,2,1,0:T(8,128)S(1)} %shard_map.48.p_in.after_ref), custom_call_target="tpu_custom_call" | custom-call | flops 1048576 | bytes 1048576 | tf_op jit(solution)/shard_map/pallas_call | solution.py:738
  6.1 0.7 %collective-permute-start.3 = (f32[4,56,128]{2,1,0:T(8,128)S(1)}, f32[4,56,128]{2,1,0:T(8,128)S(1)}, u32[]{:S(2)}, u32[]{:S(2)}) collective-permute-start(f32[4,56,128]{2,1,0:T(8,128)S(1)} %get-tuple-element.40), channel_id=1, source_target_pairs={{64,0},{33,1},{98,2},{115,3},{68,4},{37,5},{102,6},{119,7},{72,8},... | collective-permute-start | bytes 344072 | tf_op jit(solution)/shard_map/ppermute | solution.py:691
  6.8 1.3 %collective-permute-start.4 = (f32[4,56,128]{2,1,0:T(8,128)S(1)}, f32[4,56,128]{2,1,0:T(8,128)S(1)}, u32[]{:S(2)}, u32[]{:S(2)}) collective-permute-start(f32[4,56,128]{2,1,0:T(8,128)S(1)} %get-tuple-element.40), channel_id=1, source_target_pairs={{128,0},{145,1},{162,2},{179,3},{132,4},{149,5},{166,6},{183,7},{1... | collective-permute-start | bytes 344072 | tf_op jit(solution)/shard_map/ppermute | solution.py:691
  8.1 0.7 %collective-permute-start.5 = (f32[4,56,128]{2,1,0:T(8,128)S(1)}, f32[4,56,128]{2,1,0:T(8,128)S(1)}, u32[]{:S(2)}, u32[]{:S(2)}) collective-permute-start(f32[4,56,128]{2,1,0:T(8,128)S(1)} %get-tuple-element.40), channel_id=1, source_target_pairs={{192,0},{49,1},{226,2},{243,3},{196,4},{53,5},{230,6},{247,7},{200... | collective-permute-start | bytes 344072 | tf_op jit(solution)/shard_map/ppermute | solution.py:691
  8.8 0.0 copy-done.6
  8.8 0.0 copy-done.1
  8.8 1.7 %shard_map.47 = (f32[4,48,16,128]{3,2,1,0:T(8,128)S(1)}, bf16[48,16,128]{2,1,0:T(8,128)(2,1)S(1)}, bf16[3,256,128]{2,1,0:T(8,128)(2,1)S(1)}, f32[8,128]{1,0:T(8,128)S(1)}) custom-call(f32[4,48,16,128]{3,2,1,0:T(8,128)S(1)} %copy-done.1, s32[8,128]{1,0:T(8,128)S(1)} %pad.4.fp_ref), custom_call_target="tpu_custom_call" | custom-call | flops 1048576 | bytes 1048576 | tf_op jit(solution)/shard_map/pallas_call | solution.py:743
  10.5 0.0 copy-start.4
  10.5 1.1 %copy-done.4 = f32[4,48,16,128]{3,2,1,0:T(8,128)} copy-done((f32[4,48,16,128]{3,2,1,0:T(8,128)}, f32[4,48,16,128]{3,2,1,0:T(8,128)S(1)}, u32[]{:S(2)}) %copy-start.4) | copy-done | bytes 1572888
  11.6 6.5 %collective-permute-done.1.rb_ref = f32[48,8,128]{2,1,0:T(8,128)S(1)} collective-permute-done((f32[48,8,128]{2,1,0:T(8,128)S(1)}, f32[48,8,128]{2,1,0:T(8,128)S(1)}, u32[]{:S(2)}, u32[]{:S(2)}) %collective-permute-start.1) | collective-permute-done | bytes 196640 | tf_op jit(solution)/shard_map/ppermute | solution.py:727
  18.1 0.7 %collective-permute-start.2 = (f32[4,56,128]{2,1,0:T(8,128)S(1)}, f32[4,56,128]{2,1,0:T(8,128)S(1)}, u32[]{:S(2)}, u32[]{:S(2)}) collective-permute-start(f32[4,56,128]{2,1,0:T(8,128)S(1)} %get-tuple-element.40), channel_id=1, source_target_pairs={{17,1},{82,2},{211,3},{21,5},{86,6},{215,7},{25,9},{90,10},{219,11... | collective-permute-start | bytes 344072 | tf_op jit(solution)/shard_map/ppermute | solution.py:691
  18.8 0.1 fusion
  18.9 0.0 collective-permute-done.ra_ref
  18.9 0.9 %shard_map.49 = (f32[2,4,24,128]{3,2,1,0:T(8,128)S(1)}, f32[48,8,128]{2,1,0:T(8,128)S(1)}, f32[48,8,128]{2,1,0:T(8,128)S(1)}, f32[48,8,128]{2,1,0:T(8,128)S(1)}) custom-call(f32[48,8,128]{2,1,0:T(8,128)S(1)} %get-tuple-element.27.after_ref.sa_ref, f32[48,8,128]{2,1,0:T(8,128)S(1)} %get-tuple-element.32.sb_ref, ...), custom_call_target="tpu_custom_call" | custom-call | flops 1048576 | bytes 1048576 | tf_op jit(solution)/shard_map/pallas_call | solution.py:756
  19.8 0.5 %collective-permute-start.6 = (f32[2,4,24,128]{3,2,1,0:T(8,128)S(1)}, f32[2,4,24,128]{3,2,1,0:T(8,128)S(1)}, u32[]{:S(2)}, u32[]{:S(2)}) collective-permute-start(f32[2,4,24,128]{3,2,1,0:T(8,128)S(1)} %get-tuple-element.37.p_ref), channel_id=1, source_target_pairs={{0,15},{1,2},{2,1},{3,4},{4,3},{5,6},{6,5},{7,8},{8,7},{9,10},{10,... | collective-permute-start | bytes 294920 | tf_op jit(solution)/shard_map/ppermute | solution.py:759
  20.3 0.8 %fusion.3 = (s32[128]{0:T(128)S(1)}, s32[128]{0:T(128)S(1)}, s32[128]{0:T(128)S(1)}) fusion(s32[3,100]{1,0:T(4,128)} %bitcast.49), kind=kLoop, calls=%fused_computation.31 | loop fusion | bytes 2736 | tf_op jit(solution)/shard_map/sub | solution.py:733
  21.1 0.0 collective-permute-done.3
  21.1 0.0 collective-permute-done.4
  21.1 0.0 collective-permute-done.5
  21.1 4.9 %collective-permute-done.6.pb_ref = f32[2,4,24,128]{3,2,1,0:T(8,128)S(1)} collective-permute-done((f32[2,4,24,128]{3,2,1,0:T(8,128)S(1)}, f32[2,4,24,128]{3,2,1,0:T(8,128)S(1)}, u32[]{:S(2)}, u32[]{:S(2)}) %collective-permute-start.6) | collective-permute-done | bytes 98336 | tf_op jit(solution)/shard_map/ppermute | solution.py:759
  26.0 0.0 collective-permute-done.2
  26.1 0.0 copy-start.5
  26.1 0.1 collective-permute-start.7
  26.3 0.1 multiply_select_fusion.lap_ref
  26.4 1.5 %collective-permute-done.7 = f32[640,128]{1,0:T(8,128)S(1)} collective-permute-done((f32[640,128]{1,0:T(8,128)S(1)}, f32[640,128]{1,0:T(8,128)S(1)}, u32[]{:S(2)}, u32[]{:S(2)}) %collective-permute-start.7) | collective-permute-done | bytes 327712 | tf_op jit(solution)/shard_map/ppermute | solution.py:705
  27.9 0.1 collective-permute-start.8
  28.0 0.0 copy-done.5
  28.1 3.4 %shard_map.51 = (f32[4,48,16,128]{3,2,1,0:T(8,128)}, f32[48,8,128]{2,1,0:T(8,128)S(1)}, f32[2,8,128]{2,1,0:T(8,128)S(1)}, f32[48,8,128]{2,1,0:T(8,128)S(1)}) custom-call(f32[4,48,16,128]{3,2,1,0:T(8,128)S(1)} %copy-done.1, f32[4,48,16,128]{3,2,1,0:T(8,128)S(1)} %copy-done.5, bf16[48,16,128]{2,1,0:T(8,128)(2,1)S(1)} %get-tuple-element.30.disks_ref, ...), custom_call_target="tpu_custom_call" | custom-call | flops 4294967296 | bytes 1048576 | tf_op jit(solution)/shard_map/pallas_call | solution.py:762
  31.4 1.8 %collective-permute-done.8 = f32[4,56,128]{2,1,0:T(8,128)S(1)} collective-permute-done((f32[4,56,128]{2,1,0:T(8,128)S(1)}, f32[4,56,128]{2,1,0:T(8,128)S(1)}, u32[]{:S(2)}, u32[]{:S(2)}) %collective-permute-start.8) | collective-permute-done | bytes 114720 | tf_op jit(solution)/shard_map/ppermute | solution.py:710
  33.2 0.1 shard_map.52
  (9 shorter events, 0.2 us)
Async XLA Ops:
  0.0 1.4 %copy-start = (f32[4,48,16,128]{3,2,1,0:T(8,128)S(1)}, f32[4,48,16,128]{3,2,1,0:T(8,128)}, u32[]{:S(2)}) copy-start(f32[4,48,16,128]{3,2,1,0:T(8,128)} %f_ref.7) | copy-start | bytes 4718596
  1.6 17.3 %collective-permute-start = (f32[48,8,128]{2,1,0:T(8,128)S(1)}, f32[48,8,128]{2,1,0:T(8,128)S(1)}, u32[]{:S(2)}, u32[]{:S(2)}) collective-permute-start(f32[48,8,128]{2,1,0:T(8,128)S(1)} %get-tuple-element.27.after_ref.sa_ref), channel_id=1, source_target_pairs={{0,16},{16,0},{32,48},{48,32},{64,80},{80,64},{96,112},{112,96},{1... | collective-permute-start | bytes 589832 | tf_op jit(solution)/shard_map/ppermute | solution.py:726
  3.3 2.0 %copy-start.2 = (f32[4,48,128]{2,1,0:T(8,128)S(1)}, f32[4,48,128]{2,1,0:T(8,128)}, u32[]{:S(2)}) copy-start(f32[4,48,128]{2,1,0:T(8,128)} %in_ref.1) | copy-start | bytes 294916
  3.3 2.0 %copy-start.3 = (s32[16]{0:T(128)S(1)}, s32[16]{0:T(128)}, u32[]{:S(2)}) copy-start(s32[16]{0:T(128)} %map_ref.1) | copy-start | bytes 196
  3.3 5.5 %copy-start.6 = (s32[100,3]{0,1:T(4,128)S(1)}, s32[100,3]{0,1:T(4,128)}, u32[]{:S(2)}) copy-start(s32[100,3]{0,1:T(4,128)} %param.6) | copy-start | bytes 3604
  3.3 5.5 %copy-start.1 = (f32[4,48,16,128]{3,2,1,0:T(8,128)S(1)}, f32[4,48,16,128]{3,2,1,0:T(8,128)}, u32[]{:S(2)}) copy-start(f32[4,48,16,128]{3,2,1,0:T(8,128)} %f_ref.7) | copy-start | bytes 4718596
  3.3 14.8 %collective-permute-start.1 = (f32[48,8,128]{2,1,0:T(8,128)S(1)}, f32[48,8,128]{2,1,0:T(8,128)S(1)}, u32[]{:S(2)}, u32[]{:S(2)}) collective-permute-start(f32[48,8,128]{2,1,0:T(8,128)S(1)} %get-tuple-element.32.sb_ref), channel_id=1, source_target_pairs={{0,1},{1,0},{2,3},{3,2},{4,5},{5,4},{6,7},{7,6},{8,9},{9,8},{10,11... | collective-permute-start | bytes 589832 | tf_op jit(solution)/shard_map/ppermute | solution.py:727
  6.1 15.0 %collective-permute-start.3 = (f32[4,56,128]{2,1,0:T(8,128)S(1)}, f32[4,56,128]{2,1,0:T(8,128)S(1)}, u32[]{:S(2)}, u32[]{:S(2)}) collective-permute-start(f32[4,56,128]{2,1,0:T(8,128)S(1)} %get-tuple-element.40), channel_id=1, source_target_pairs={{64,0},{33,1},{98,2},{115,3},{68,4},{37,5},{102,6},{119,7},{72,8},... | collective-permute-start | bytes 344072 | tf_op jit(solution)/shard_map/ppermute | solution.py:691
  6.8 14.3 %collective-permute-start.4 = (f32[4,56,128]{2,1,0:T(8,128)S(1)}, f32[4,56,128]{2,1,0:T(8,128)S(1)}, u32[]{:S(2)}, u32[]{:S(2)}) collective-permute-start(f32[4,56,128]{2,1,0:T(8,128)S(1)} %get-tuple-element.40), channel_id=1, source_target_pairs={{128,0},{145,1},{162,2},{179,3},{132,4},{149,5},{166,6},{183,7},{1... | collective-permute-start | bytes 344072 | tf_op jit(solution)/shard_map/ppermute | solution.py:691
  8.1 13.0 %collective-permute-start.5 = (f32[4,56,128]{2,1,0:T(8,128)S(1)}, f32[4,56,128]{2,1,0:T(8,128)S(1)}, u32[]{:S(2)}, u32[]{:S(2)}) collective-permute-start(f32[4,56,128]{2,1,0:T(8,128)S(1)} %get-tuple-element.40), channel_id=1, source_target_pairs={{192,0},{49,1},{226,2},{243,3},{196,4},{53,5},{230,6},{247,7},{200... | collective-permute-start | bytes 344072 | tf_op jit(solution)/shard_map/ppermute | solution.py:691
  10.5 1.1 %copy-start.4 = (f32[4,48,16,128]{3,2,1,0:T(8,128)}, f32[4,48,16,128]{3,2,1,0:T(8,128)S(1)}, u32[]{:S(2)}) copy-start(f32[4,48,16,128]{3,2,1,0:T(8,128)S(1)} %get-tuple-element.29.base_ref) | copy-start | bytes 4718596
  18.1 7.9 %collective-permute-start.2 = (f32[4,56,128]{2,1,0:T(8,128)S(1)}, f32[4,56,128]{2,1,0:T(8,128)S(1)}, u32[]{:S(2)}, u32[]{:S(2)}) collective-permute-start(f32[4,56,128]{2,1,0:T(8,128)S(1)} %get-tuple-element.40), channel_id=1, source_target_pairs={{17,1},{82,2},{211,3},{21,5},{86,6},{215,7},{25,9},{90,10},{219,11... | collective-permute-start | bytes 344072 | tf_op jit(solution)/shard_map/ppermute | solution.py:691
  19.8 6.2 %collective-permute-start.6 = (f32[2,4,24,128]{3,2,1,0:T(8,128)S(1)}, f32[2,4,24,128]{3,2,1,0:T(8,128)S(1)}, u32[]{:S(2)}, u32[]{:S(2)}) collective-permute-start(f32[2,4,24,128]{3,2,1,0:T(8,128)S(1)} %get-tuple-element.37.p_ref), channel_id=1, source_target_pairs={{0,15},{1,2},{2,1},{3,4},{4,3},{5,6},{6,5},{7,8},{8,7},{9,10},{10,... | collective-permute-start | bytes 294920 | tf_op jit(solution)/shard_map/ppermute | solution.py:759
  26.1 2.0 %copy-start.5 = (f32[4,48,16,128]{3,2,1,0:T(8,128)S(1)}, f32[4,48,16,128]{3,2,1,0:T(8,128)}, u32[]{:S(2)}) copy-start(f32[4,48,16,128]{3,2,1,0:T(8,128)} %copy-done.4) | copy-start | bytes 4718596
  26.1 1.7 %collective-permute-start.7 = (f32[640,128]{1,0:T(8,128)S(1)}, f32[640,128]{1,0:T(8,128)S(1)}, u32[]{:S(2)}, u32[]{:S(2)}) collective-permute-start(f32[640,128]{1,0:T(8,128)S(1)} %pad_maximum_fusion), channel_id=1, source_target_pairs={{0,1},{1,0},{2,3},{3,2},{4,5},{5,4},{6,7},{7,6},{8,9},{9,8},{10,11... | collective-permute-start | bytes 983048 | tf_op jit(solution)/shard_map/ppermute | solution.py:705
  27.9 5.3 %collective-permute-start.8 = (f32[4,56,128]{2,1,0:T(8,128)S(1)}, f32[4,56,128]{2,1,0:T(8,128)S(1)}, u32[]{:S(2)}, u32[]{:S(2)}) collective-permute-start(f32[4,56,128]{2,1,0:T(8,128)S(1)} %select_select_fusion), channel_id=1, source_target_pairs={{0,2},{1,3},{2,0},{3,1},{4,6},{5,7},{6,4},{7,5},{8,10},{9,11},{10,... | collective-permute-start | bytes 344072 | tf_op jit(solution)/shard_map/ppermute | solution.py:710
